TPU v7x, 512 devices: a whole 4x8x8 slice. The times are simulated.
512 devices in a mesh: dp: 16 (over z_hi, x, core), ctx: 32 (over z_lo, y).
Axes of the slice: x: 4, y: 8, z: 8 (z_hi: 2, z_lo: 4; z = z_hi * 4 + z_lo), core: 2. Of those that a mesh axis runs over, the one named last changes fastest.
Arguments:
- queries: bfloat16 [4096, 8192], P('ctx', 'dp'), may hold values from -150 to 150
- keys: bfloat16 [4096, 512], P('ctx'), may hold values from -6 to 6
- values: bfloat16 [4096, 512], P('ctx'), may hold values from -6 to 6
- grad_out: bfloat16 [4096, 8192], P('ctx', 'dp'), may hold values from -6 to 6
- spans: int32 [32, 2], replicated, may hold values from 0 to 63, as said below
Outputs:
- grad_queries: bfloat16 [4096, 8192], P('ctx', 'dp')
- grad_keys: bfloat16 [4096, 512], P('ctx', 'dp')
- grad_values: bfloat16 [4096, 512], P('ctx', 'dp')
Inputs may be any that keep to these rules, and one draw needn't show every extreme that they name: `spans`: row r holds c and 63 - c with c < 32; every span number appears exactly once in the table.
All inputs are finite; a program needn't handle non-finite values.
Results may differ from a plain program's by a relative error of at most 0.015.
Values may be sent and summed in bfloat16 or wider, within the bound.
No kernel may reach another device: no remote copies, remote signals or barrier semaphores. Data moves between devices by JAX's collectives and lax.ppermute only.
A program may use at most 64 MiB of HBM per device.

v0:
```python
import math

import jax
import jax.numpy as jnp
from jax import lax
from jax.sharding import PartitionSpec as P

HD = 128
H = 64
KVH = 4


def from_partner(shard, axis, stride):
    return lax.ppermute(shard, axis, [(i, i ^ 1 << stride) for i in range(lax.axis_size(axis))])


def on_device(queries, keys, values, grad_out, spans):
    rows = queries.shape[0]
    heads_dev = queries.shape[1] // HD
    group = H // KVH
    kv_dev = max(1, heads_dev // group)
    sharers = max(1, group // heads_dev)
    nbits = sharers.bit_length() - 1
    width = kv_dev * HD
    local_group = heads_dev // kv_dev
    dp_index = lax.axis_index("dp")
    ctx_index = lax.axis_index("ctx")
    ctx_count = lax.axis_size("ctx")
    seq_len = rows * ctx_count
    half_rows = rows // 2
    scale = 1.0 / math.sqrt(HD)
    first_kv = dp_index * heads_dev // group
    key_own = lax.dynamic_slice_in_dim(keys, first_kv * HD, width, 1)
    value_own = lax.dynamic_slice_in_dim(values, first_kv * HD, width, 1)
    key_all, value_all = (
        lax.all_gather(key_own, "ctx", axis=0, tiled=True),
        lax.all_gather(value_own, "ctx", axis=0, tiled=True),
    )
    span_flat = spans.reshape(-1)
    key_rows = jnp.arange(seq_len, dtype=jnp.int32)
    span_ids = jnp.arange(span_flat.shape[0], dtype=jnp.int32)
    owner_span = jnp.sum(
        jnp.where((key_rows // half_rows)[:, None] == span_ids[None, :], span_flat[None, :], 0),
        axis=1,
    )
    pos_key = owner_span * half_rows + key_rows % half_rows
    mine = lax.dynamic_slice_in_dim(spans, ctx_index, 1, 0).reshape(2)
    query_rows = jnp.arange(rows, dtype=jnp.int32)
    pos_query = (
        jnp.where(query_rows < half_rows, mine[0], mine[1]) * half_rows + query_rows % half_rows
    )
    query_four = queries.reshape(rows, kv_dev, local_group, HD)
    cotan_four = grad_out.reshape(rows, kv_dev, local_group, HD)
    block = math.gcd(seq_len, 512)
    nblocks = seq_len // block

    def tiles(at, size):
        key_blk = lax.dynamic_slice_in_dim(key_all, at, size, 0).reshape(size, kv_dev, HD)
        value_blk = lax.dynamic_slice_in_dim(value_all, at, size, 0).reshape(size, kv_dev, HD)
        pos_blk = lax.dynamic_slice_in_dim(pos_key, at, size, 0)
        scores = (
            jnp.einsum("rngd,bnd->ngrb", query_four, key_blk, preferred_element_type=jnp.float32)
            * scale
        )
        visible = pos_blk[None, :] <= pos_query[:, None]
        return (key_blk, value_blk, scores, visible)

    def stats(idx, carry):
        top, total = carry
        key_blk, value_blk, scores, visible = tiles(idx * block, block)
        new_top = jnp.maximum(top, jnp.max(jnp.where(visible, scores, -1e30), axis=-1))
        total = total * jnp.exp(top - new_top) + jnp.sum(
            jnp.where(visible, jnp.exp(scores - new_top[..., None]), 0.0), axis=-1
        )
        return (new_top, total)

    start_top = jnp.full((kv_dev, local_group, rows), -1e30, jnp.float32)
    top, total = lax.fori_loop(0, nblocks, stats, (start_top, jnp.zeros_like(start_top)))
    lse = top + jnp.log(total)

    def weights(scores, visible):
        return jnp.where(visible, jnp.exp(scores - lse[..., None]), 0.0)

    def outputs(idx, acc):
        key_blk, value_blk, scores, visible = tiles(idx * block, block)
        probs_b = weights(scores, visible).astype(jnp.bfloat16)
        return acc + jnp.einsum(
            "ngrb,bnd->ngrd", probs_b, value_blk, preferred_element_type=jnp.float32
        )

    output = lax.fori_loop(
        0, nblocks, outputs, jnp.zeros((kv_dev, local_group, rows, HD), jnp.float32)
    )
    delta = jnp.sum(jnp.transpose(cotan_four.astype(jnp.float32), (1, 2, 0, 3)) * output, axis=-1)

    def score_grads(scores, visible, value_blk):
        probs = weights(scores, visible)
        dprob = jnp.einsum(
            "rngd,bnd->ngrb", cotan_four, value_blk, preferred_element_type=jnp.float32
        )
        dscore = (probs * (dprob - delta[..., None])).astype(jnp.bfloat16)
        return (probs, dscore)

    def query_grads(idx, acc):
        key_blk, value_blk, scores, visible = tiles(idx * block, block)
        probs, dscore = score_grads(scores, visible, value_blk)
        return acc + jnp.einsum(
            "ngrb,bnd->rngd", dscore, key_blk, preferred_element_type=jnp.float32
        )

    grad_q = lax.fori_loop(
        0, nblocks, query_grads, jnp.zeros((rows, kv_dev, local_group, HD), jnp.float32)
    )
    grad_queries = (grad_q * scale).reshape(rows, heads_dev * HD).astype(jnp.bfloat16)
    size = math.gcd(rows * lax.axis_size("ctx"), 512)

    def one(idx, acc):
        key_blk, value_blk, scores, visible = tiles(idx * size, size)
        probs, dscore = score_grads(scores, visible, value_blk)
        probs_b = probs.astype(jnp.bfloat16)
        grad_k = (
            jnp.einsum("ngrb,rngd->bnd", dscore, query_four, preferred_element_type=jnp.float32)
            * scale
        )
        grad_v = jnp.einsum(
            "ngrb,rngd->bnd", probs_b, cotan_four, preferred_element_type=jnp.float32
        )
        term = jnp.stack((grad_k.reshape(size, width), grad_v.reshape(size, width)), axis=1)
        return lax.dynamic_update_slice_in_dim(acc, term, idx * size, 0)

    summed = lax.psum_scatter(
        lax.fori_loop(
            0,
            rows * lax.axis_size("ctx") // size,
            one,
            jnp.zeros((rows * lax.axis_size("ctx"), 2, width), jnp.float32),
        ),
        "ctx",
        scatter_dimension=0,
        tiled=True,
    )
    for bit in reversed(range(nbits)):
        middle = summed.shape[2] // 2
        lower_part = summed[:, :, :middle]
        upper_part = summed[:, :, middle:]
        upper = dp_index // 2**bit % 2 == 1
        keep = jnp.where(upper, upper_part, lower_part)
        give = jnp.where(upper, lower_part, upper_part)
        summed = keep + from_partner(give, "dp", bit)
    grad_keys = summed[:, 0, :].astype(jnp.bfloat16)
    grad_values = summed[:, 1, :].astype(jnp.bfloat16)
    return (grad_queries, grad_keys, grad_values)


def solution(mesh):
    return jax.shard_map(
        on_device,
        mesh=mesh,
        in_specs=(P("ctx", "dp"), P("ctx", None), P("ctx", None), P("ctx", "dp"), P()),
        out_specs=(P("ctx", "dp"), P("ctx", "dp"), P("ctx", "dp")),
        check_vma=False,
    )
```

profile of v0, /device:TPU:1, one launch (start us, length us, event | category | flops | bytes accessed | tf_op | source)
XLA Modules:
  0.0 606.1 jit_solution(18310388527986604092)
XLA Ops:
  8.8 1.4 constant_dynamic-slice_fusion
  15.1 133.1 %all-gather.3.cloned.1.call-done = bf16[4096,128]{1,0:T(8,128)(2,1)} async-done(((bf16[128,128]{1,0:T(8,128)(2,1)}), bf16[4096,128]{1,0:T(8,128)(2,1)}) %all-gather.3.cloned.1.call-update) | async-done | bytes 1048592 | tf_op jit(solution)/shard_map/all_gather | solution.py:36
  148.2 23.8 %while.59 = (s32[]{:T(128)}, f32[1,4,128]{2,1,0:T(4,128)S(1)}, f32[1,4,128]{2,1,0:T(4,128)S(1)}, s32[4096]{0:T(1024)S(1)}, bf16[4096,128]{1,0:T(8,128)(2,1)}, /*...) while((s32[]{:T(128)}, f32[1,4,128]{2,1,0:T(4,128)S(1)}, ...), condition=%wide.region_4.5_spmd.clone, body=%wide.region_1.4_spmd.clone.sunk | while | flops 68751112 | bytes 2589886 | solution.py:78
  172.0 126.2 %all-gather.5.cloned.1.call-done = bf16[4096,128]{1,0:T(8,128)(2,1)} async-done(((bf16[128,128]{1,0:T(8,128)(2,1)}), bf16[4096,128]{1,0:T(8,128)(2,1)}) %all-gather.5.cloned.1.call-update) | async-done | bytes 1048592 | tf_op jit(solution)/shard_map/all_gather | solution.py:37
  298.2 25.3 %while.60 = (s32[]{:T(128)}, f32[1,4,128,128]{3,2,1,0:T(8,128)S(1)}, s32[4096]{0:T(1024)S(1)}, bf16[4096,128]{1,0:T(8,128)(2,1)}, bf16[128,1,4,128]{3,0,2,1:T(8,...) while((s32[]{:T(128)}, ...), condition=%wide.region_6.7_spmd.clone, body=%wide.region_5.6_spmd.clone.sunk | while | flops 135464192 | bytes 1059520 | solution.py:91
  299.7 1.7 fusion.144
  302.8 1.7 fusion.144
  306.0 1.7 fusion.144
  309.2 1.7 fusion.144
  312.3 1.7 fusion.144
  315.5 1.7 fusion.144
  318.7 1.7 fusion.144
  321.8 1.7 fusion.144
  323.7 2.4 broadcast_in_dim.156.clone
  326.1 45.2 %while.58 = (s32[]{:T(128)}, f32[4096,2,128]{0,2,1:T(8,128)}, s32[4096]{0:T(1024)S(1)}, bf16[4096,128]{1,0:T(8,128)(2,1)}, bf16[128,1,4,128]{3,0,2,1:T(8,128)(2,...) while((s32[]{:T(128)}, f32[4096,2,128]{0,2,1:T(8,128)}, ...), condition=%wide.region_11.12_spmd.clone, body=%wide.region_10.11_spmd.clone.sunk | while | flops 270533888 | bytes 7744723 | solution.py:132
  327.6 1.3 fusion.137
  328.9 1.5 fusion.138
  333.2 1.3 fusion.137
  334.5 1.5 fusion.138
  338.9 1.3 fusion.137
  340.1 1.5 fusion.138
  344.5 1.3 fusion.137
  345.8 1.4 fusion.138
  350.2 1.3 fusion.137
  351.5 1.4 fusion.138
  355.8 1.3 fusion.137
  357.1 1.5 fusion.138
  361.5 1.3 fusion.137
  362.8 1.4 fusion.138
  367.1 1.3 fusion.137
  368.4 1.5 fusion.138
  371.4 163.0 %reduce-scatter.2.cloned.1.call-done = f32[128,2,128]{0,2,1:T(8,128)} async-done(((f32[4096,2,128]{0,2,1:T(8,128)}), f32[128,2,128]{0,2,1:T(8,128)}) %reduce-scatter.2.cloned.1.call-update) | async-done | bytes 131088 | tf_op jit(solution)/shard_map/reduce_scatter | solution.py:131
  535.3 2.7 collective-permute-start
  538.0 34.2 %while.61 = (s32[]{:T(128)}, f32[128,1,4,128]{0,3,2,1:T(8,128)S(1)}, bf16[4096,128]{1,0:T(8,128)(2,1)}, s32[4096]{0:T(1024)S(1)}, bf16[128,1,4,128]{3,0,2,1:T(8,...) while((s32[]{:T(128)}, ...), condition=%wide.region_9.10_spmd.clone, body=%wide.region_8.9_spmd.clone.sunk | while | flops 203097344 | bytes 3420884 | solution.py:111
  539.5 1.3 fusion.151
  540.8 1.5 fusion.152
  543.8 1.3 fusion.151
  545.1 1.5 fusion.152
  548.1 1.3 fusion.151
  549.4 1.5 fusion.152
  553.6 1.5 fusion.152
  556.6 1.3 fusion.151
  557.9 1.5 fusion.152
  560.9 1.3 fusion.151
  562.2 1.5 fusion.152
  566.4 1.5 fusion.152
  570.7 1.5 fusion.152
  572.3 25.9 %collective-permute-start.1 = (f32[128,2,32]{0,2,1:T(8,128)S(1)}, f32[128,2,32]{0,2,1:T(8,128)S(1)}, u32[]{:S(2)}, u32[]{:S(2)}) collective-permute-start(f32[128,2,32]{0,2,1:T(8,128)S(1)} %slice_select_fusion.1), channel_id=1, source_target_pairs={{0,32},{32,0},{64,96},{96,64},{128,160},{160,128},{192,224},{224,1... | collective-permute-start | bytes 98312 | tf_op jit(solution)/shard_map/ppermute | solution.py:14
  (209 shorter events, 82.7 us)
Async XLA Ops:
  7.2 0.9 copy-start
  7.2 141.0 %all-gather.3.cloned.1.call-start = ((), (), s32[]{:S(2)}) async-start(), calls=%async_computation.1 | async-start | bytes 1081344 | tf_op jit(solution)/shard_map/all_gather | solution.py:36
  8.7 289.5 %all-gather.5.cloned.1.call-start = ((), (), s32[]{:S(2)}) async-start(), calls=%async_computation.2 | async-start | bytes 1081344 | tf_op jit(solution)/shard_map/all_gather | solution.py:37
  10.2 524.3 %reduce-scatter.2.cloned.1.call-start = ((), (), s32[]{:S(2)}) async-start(), calls=%async_computation.3 | async-start | bytes 4325376 | tf_op jit(solution)/shard_map/reduce_scatter | solution.py:131
  535.3 36.9 %collective-permute-start = (f32[128,2,64]{0,2,1:T(8,128)S(1)}, f32[128,2,64]{0,2,1:T(8,128)S(1)}, u32[]{:S(2)}, u32[]{:S(2)}) collective-permute-start(f32[128,2,64]{0,2,1:T(8,128)S(1)} %slice_select_fusion), channel_id=1, source_target_pairs={{0,64},{32,96},{64,0},{96,32},{128,192},{160,224},{192,128},{224,1... | collective-permute-start | bytes 196616 | tf_op jit(solution)/shard_map/ppermute | solution.py:14
  538.0 34.2 %copy-start.1 = (f32[128,2,128]{0,2,1:T(8,128)S(1)}, f32[128,2,128]{0,2,1:T(8,128)}, u32[]{:S(2)}) copy-start(f32[128,2,128]{0,2,1:T(8,128)} %reduce-scatter.2.cloned.1.call-done) | copy-start | bytes 393220
  572.3 26.7 %collective-permute-start.1 = (f32[128,2,32]{0,2,1:T(8,128)S(1)}, f32[128,2,32]{0,2,1:T(8,128)S(1)}, u32[]{:S(2)}, u32[]{:S(2)}) collective-permute-start(f32[128,2,32]{0,2,1:T(8,128)S(1)} %slice_select_fusion.1), channel_id=1, source_target_pairs={{0,32},{32,0},{64,96},{96,64},{128,160},{160,128},{192,224},{224,1... | collective-permute-start | bytes 98312 | tf_op jit(solution)/shard_map/ppermute | solution.py:14
Sparse Core Ops, SparseCore 0:
  10.7 137.4 all-gather.2
  150.2 147.9 all-gather.4
  371.5 162.8 reduce-scatter.1
where the time goes:
time: 608 us; the launch traced here: 606 us
  waiting for transfers between devices  422 us (69%)
  matrix products  69.1 us (11%)
  other arithmetic  48 us (8%)
  starting transfers between devices  28.7 us (5%)
  local copies, waits for them, and re-layouts  22.3 us (4%)
  between operations  14 us (2%)
    reduce_scatter x1, waiting for transfers between devices, on_device(): lax.psum_scatter(lax.fori_loop(0, rows * lax.axis_size('ctx') // size, on...  163 us
    all_gather x1, waiting for transfers between devices, on_device(): lax.all_gather(key_own, 'ctx', axis=0, tiled=True)  133 us
    all_gather x1, waiting for transfers between devices, on_device(): lax.all_gather(value_own, 'ctx', axis=0, tiled=True)  126 us
    add x32, other arithmetic, on_device(): jnp.where(query_rows < half_rows, mine[0], mine[1]) * half_rows  40.1 us
    dot_general x24, matrix products, tiles(): jnp.einsum('rngd,bnd->ngrb', query_four, key_blk, preferred_element_type=...  29.9 us
    ppermute x2, starting transfers between devices, from_partner(): lax.ppermute(shard, axis, [(i, i ^ 1 << stride) for i in range(lax.axis_s...  28.6 us
    dot_general x8, matrix products, outputs(): jnp.einsum('ngrb,bnd->ngrd', probs_b, value_blk, preferred_element_type=j...  13.2 us
  transfers between devices with their start and end apart: 5, of which 3 were waited for; matrix products, arithmetic and copies ran while one was open for 11% of the time, Pallas kernels for 0%

commit v1 on v0

v1 whole, which is shorter than its diff:
```python
import functools
import math

import jax
import jax.numpy as jnp
from jax import lax
from jax.experimental import pallas as pl
from jax.experimental.pallas import tpu as pltpu
from jax.sharding import Mesh
from jax.sharding import PartitionSpec as P

HD = 128
H = 64
KVH = 4
SPAN = 64
SUB = 16
TILE = 256
LOW = -1e30
FLOOR = -1e29
SCALE = 1.0 / math.sqrt(HD)
EXP2 = SCALE * math.log2(math.e)
VM = pltpu.VMEM
F32 = jnp.float32
BF16 = jnp.bfloat16
NT = (((1,), (1,)), ((), ()))
NN = (((1,), (0,)), ((), ()))


def dot(a, b, dims=NN):
    return lax.dot_general(a, b, dims, preferred_element_type=F32)


def pick_kernel(meta, keys, values, kv_out, held, sems):
    col = pl.multiple_of(meta[0] * HD, HD)
    copies = []
    for which, ref in enumerate((keys, values)):
        for half in range(2):
            at = which * 2 + half
            row = pl.multiple_of(half * SPAN + meta[1] * SUB, SUB)
            copies.append(
                pltpu.make_async_copy(
                    ref.at[pl.ds(row, SUB), pl.ds(col, HD)], held.at[at * SUB : (at + 1) * SUB, :], sems.at[at]
                )
            )
    for copy in copies:
        copy.start()
    for copy in copies:
        copy.wait()
    for dest in range(kv_out.shape[0]):
        kv_out[dest] = held[...]


def pair_kernel(queries, cotan, out):
    out[0] = queries[...]
    out[1] = cotan[...]


def load(meta, spans, kv, own, other, ks, vs, qs, gs):
    for src in range(kv.shape[0]):
        for half in range(2):
            at = pl.multiple_of(spans[src, half] * SUB, SUB)
            ks[pl.ds(at, SUB), :] = kv[src, half * SUB : (half + 1) * SUB, :]
            vs[pl.ds(at, SUB), :] = kv[src, (2 + half) * SUB : (3 + half) * SUB, :]
    heads = own.shape[3] // HD
    for pair, ref in enumerate((own, other)):
        for core in range(2):
            for head in range(heads):
                at = (((pair ^ meta[4]) * 2 + core) * heads + head) * SPAN
                at = pl.multiple_of(at, SPAN)
                for half in range(2):
                    rows = slice(half * SPAN, (half + 1) * SPAN)
                    cols = slice(head * HD, (head + 1) * HD)
                    rank = half ^ meta[5]
                    qs[rank, pl.ds(at, SPAN), :] = ref[core, 0, rows, cols]
                    gs[rank, pl.ds(at, SPAN), :] = ref[core, 1, rows, cols]


def offsets(width):
    key = lax.broadcasted_iota(jnp.int32, (TILE, width), 0)
    row = lax.broadcasted_iota(jnp.int32, (TILE, width), 1)
    return (key // SUB) * SPAN + key % SUB - row % SPAN


def units(meta):
    early = meta[2] < 16
    return (
        (0, 0, True),
        (1, 0, False),
        (1, 1, False),
        (1, 2, True),
        (jnp.where(early, 1, 0), jnp.where(early, 3, 1), True),
    )


def bound(meta, half, tile):
    span = jnp.where(half == 0, meta[2], meta[3])
    return span * SPAN - tile * (TILE // SUB * SPAN) - meta[1] * SUB


WIDTH = 256


def stats_kernel(meta, spans, kv, own, other, out, ks, vs, qs, gs, part):
    load(meta, spans, kv, own, other, ks, vs, qs, gs)
    rows = qs.shape[1]
    for unit, (half, tile, masked) in enumerate(units(meta)):
        at = pl.multiple_of(tile * TILE, TILE) if unit == 4 else tile * TILE
        key = ks[pl.ds(at, TILE), :]
        value = vs[pl.ds(at, TILE), :]
        for first in range(0, rows, WIDTH):
            cols = slice(first, first + WIDTH)
            score = dot(key, qs[half, cols, :], NT)
            if masked:
                score = jnp.where(offsets(WIDTH) <= bound(meta, half, tile), score, LOW)
            top = jnp.maximum(jnp.max(score, axis=0, keepdims=True), FLOOR)
            weight = jnp.exp2((score - top) * EXP2)
            dprob = dot(value, gs[half, cols, :], NT)
            part[unit, 0:1, cols] = top
            part[unit, 1:2, cols] = jnp.sum(weight, axis=0, keepdims=True)
            part[unit, 2:3, cols] = jnp.sum(weight * dprob, axis=0, keepdims=True)
    early = meta[2] < 16
    for half, mine in enumerate(((0,), (1, 2, 3))):
        extra = jnp.where(early, F32(half), F32(1 - half)) > 0.5
        tops = [part[unit, 0:1, :] for unit in mine] + [jnp.where(extra, part[4, 0:1, :], FLOOR)]
        top = functools.reduce(jnp.maximum, tops)
        total = jnp.zeros_like(top)
        weighted = jnp.zeros_like(top)
        for unit, unit_top in zip(mine + (4,), tops):
            factor = jnp.exp2((unit_top - top) * EXP2)
            if unit == 4:
                factor = jnp.where(extra, factor, 0.0)
            total = total + factor * part[unit, 1:2, :]
            weighted = weighted + factor * part[unit, 2:3, :]
        out[half * 3 : half * 3 + 1, :] = top
        out[half * 3 + 1 : half * 3 + 2, :] = total
        out[half * 3 + 2 : half * 3 + 3, :] = weighted
    out[6:8, :] = jnp.zeros((2, rows), F32)


def sort_keys(spans, kv, first, out):
    for src in range(kv.shape[0]):
        for half in range(2):
            at = pl.multiple_of(spans[src, half] * SUB, SUB)
            out[pl.ds(at, SUB), :] = kv[src, (first + half) * SUB : (first + half + 1) * SUB, :]


def key_grads_kernel(
    meta, spans, stats, kv, own, other, dkv_out, dscore_out,
    ks, vs, qs, gs, row_stats, probs_b, dk, dv,
):
    load(meta, spans, kv, own, other, ks, vs, qs, gs)
    rows = qs.shape[1]
    for half in range(2):
        tops = [stats[src, half * 3 : half * 3 + 1, :] for src in range(4)]
        top = functools.reduce(jnp.maximum, tops)
        factors = [jnp.exp2((one - top) * EXP2) for one in tops]
        total = sum(factors[src] * stats[src, half * 3 + 1 : half * 3 + 2, :] for src in range(4))
        weighted = sum(factors[src] * stats[src, half * 3 + 2 : half * 3 + 3, :] for src in range(4))
        row_stats[half, 0:1, :] = top
        row_stats[half, 1:2, :] = 1.0 / total
        row_stats[half, 2:3, :] = weighted / total
    dk[3 * TILE :, :] = jnp.zeros((TILE, HD), F32)
    dv[3 * TILE :, :] = jnp.zeros((TILE, HD), F32)
    for unit, (half, tile, masked) in enumerate(units(meta)):
        at = pl.multiple_of(tile * TILE, TILE) if unit == 4 else tile * TILE
        key = ks[pl.ds(at, TILE), :]
        value = vs[pl.ds(at, TILE), :]
        for first in range(0, rows, WIDTH):
            cols = slice(first, first + WIDTH)
            score = dot(key, qs[half, cols, :], NT)
            if masked:
                score = jnp.where(offsets(WIDTH) <= bound(meta, half, tile), score, LOW)
            prob = jnp.exp2((score - row_stats[half, 0:1, cols]) * EXP2) * row_stats[half, 1:2, cols]
            dprob = dot(value, gs[half, cols, :], NT)
            dscore = prob * (dprob - row_stats[half, 2:3, cols])
            probs_b[unit % 2, :, cols] = prob.astype(BF16)
            dscore_out[unit, :, cols] = dscore.astype(BF16)
        dv_tile = dot(probs_b[unit % 2], gs[half])
        dk_tile = dot(dscore_out[unit], qs[half])
        keys_of = pl.ds(at, TILE)
        if unit in (0, 2, 3):
            dv[keys_of, :] = dv_tile
            dk[keys_of, :] = dk_tile
        else:
            dv[keys_of, :] += dv_tile
            dk[keys_of, :] += dk_tile
    for dest in range(dkv_out.shape[0]):
        for half in range(2):
            at = pl.multiple_of(spans[dest, half] * SUB, SUB)
            dkv_out[dest, half * SUB : (half + 1) * SUB, :] = (dk[pl.ds(at, SUB), :] * SCALE).astype(BF16)
            dkv_out[dest, (2 + half) * SUB : (3 + half) * SUB, :] = dv[pl.ds(at, SUB), :].astype(BF16)


def query_grads_kernel(meta, spans, kv, dscore, out_0, out_1, out_2, out_3, ks, kt, dq, back):
    sort_keys(spans, kv, 0, ks)
    kt[...] = ks[...].T
    for unit, (half, tile, _) in enumerate(units(meta)):
        at = pl.multiple_of(tile * TILE, TILE) if unit == 4 else tile * TILE
        dq_half = dot(kt[:, pl.ds(at, TILE)], dscore[unit])
        if unit in (0, 1):
            dq[half] = dq_half
        else:
            dq[half] += dq_half
    heads = out_0.shape[1] // HD
    for half in range(2):
        back[...] = (dq[half ^ meta[5]] * SCALE).T.astype(BF16)
        for step, out in enumerate((out_0, out_1, out_2, out_3)):
            for head in range(heads):
                at = pl.multiple_of(((meta[1] ^ step) * heads + head) * SPAN, SPAN)
                out[half * SPAN : (half + 1) * SPAN, head * HD : (head + 1) * HD] = back[pl.ds(at, SPAN), :]


def split_kernel(whole, sharer, grad_keys, grad_values):
    wide = grad_keys.shape[1]
    for which, out in enumerate((grad_keys, grad_values)):
        for half in range(2):
            for src in range(4):
                at = (which * 2 + half) * SUB
                block = whole[src, at : at + SUB, :]
                part = block[:, 3 * wide :]
                for mine in range(3):
                    part = jnp.where(sharer[0] == mine, block[:, mine * wide : (mine + 1) * wide], part)
                row = half * SPAN + src * SUB
                out[row : row + SUB, :] = part


def call(kernel, out_shape, scratch, flops, spaces, *args, limit=32):
    return pl.pallas_call(
        kernel,
        out_shape=out_shape,
        in_specs=[pl.BlockSpec(memory_space={"s": pltpu.SMEM, "v": VM, "a": pl.ANY}[space]) for space in spaces],
        out_specs=jax.tree.map(lambda _: pl.BlockSpec(memory_space=VM), out_shape),
        scratch_shapes=scratch,
        cost_estimate=pl.CostEstimate(flops=flops, bytes_accessed=1 << 20, transcendentals=0),
        compiler_params=pltpu.CompilerParams(vmem_limit_bytes=limit << 20),
    )(*args)


def on_device(queries, keys, values, grad_out, spans):
    rows, width = queries.shape
    ctx_count = lax.axis_size("ctx")
    group_index = lax.axis_index("group")
    x_index = lax.axis_index("pair")
    sharer = x_index * 2 + lax.axis_index("core")
    ctx_index = lax.axis_index("ctx")
    mine = lax.dynamic_slice_in_dim(spans, ctx_index, 1, 0).reshape(2)
    low, high = jnp.minimum(mine[0], mine[1]), jnp.maximum(mine[0], mine[1])
    meta = jnp.stack((group_index, sharer, low, high, x_index, mine[0] > mine[1])).astype(jnp.int32)
    pick_meta = jnp.stack((group_index, sharer)).astype(jnp.int32)
    sds = jax.ShapeDtypeStruct
    blocks = sds((ctx_count, 4 * SUB, HD), BF16)
    kv_send = call(
        pick_kernel,
        blocks,
        [VM((4 * SUB, HD), BF16), pltpu.SemaphoreType.DMA((4,))],
        1 << 20,
        "saa",
        pick_meta, keys, values,
        limit=60,
    )
    kv = lax.all_to_all(kv_send, "ctx", 0, 0, tiled=True)
    qd = call(pair_kernel, sds((2, rows, width), BF16), [], 1 << 20, "vv", queries, grad_out)
    crossed = lax.ppermute(qd, "pair", [(0, 1), (1, 0)])
    own = lax.all_gather(qd, "core", axis=0)
    other = lax.all_gather(crossed, "core", axis=0)
    stacked = 2 * 2 * (width // HD) * SPAN
    keys_held = 2 * ctx_count * SUB
    common = [VM((keys_held, HD), BF16)] * 2 + [VM((2, stacked, HD), BF16)] * 2
    stats = call(
        stats_kernel,
        sds((8, stacked), F32),
        common + [VM((5, 8, stacked), F32)],
        1 << 30,
        "ssvvv",
        meta, spans, kv, own, other,
    )
    stats_all = lax.all_gather(stats, ("pair", "core"), axis=0)
    dkv_send, dscore = call(
        key_grads_kernel,
        (blocks, sds((5, TILE, stacked), BF16)),
        common
        + [
            VM((2, 8, stacked), F32),
            VM((2, TILE, stacked), BF16),
            VM((keys_held, HD), F32),
            VM((keys_held, HD), F32),
        ],
        1 << 31,
        "ssvvvv",
        meta, spans, stats_all, kv, own, other,
    )
    dkv = lax.all_to_all(dkv_send, "ctx", 0, 0, tiled=True)
    dq_mine, *dq_send = call(
        query_grads_kernel,
        (sds((rows, width), BF16),) * 4,
        [
            VM((keys_held, HD), BF16),
            VM((HD, keys_held), BF16),
            VM((2, HD, stacked), F32),
            VM((stacked, HD), BF16),
        ],
        1 << 31,
        "ssvv",
        meta, spans, kv, dscore,
    )
    grad_queries = dq_mine.astype(F32)
    for step, piece in enumerate(dq_send, 1):
        grad_queries += lax.ppermute(piece, ("pair", "core"), [(i, i ^ step) for i in range(4)]).astype(F32)
    grad_queries = grad_queries.astype(BF16)
    summed = jnp.sum(dkv.astype(F32), axis=0).astype(BF16)
    whole = lax.all_gather(summed, ("pair", "core"), axis=0)
    part = sds((rows, HD // 4), BF16)
    grad_keys, grad_values = call(split_kernel, (part, part), [], 1 << 20, "vs", whole, sharer.reshape(1), limit=60)
    return (grad_queries, grad_keys, grad_values)


def solution(mesh):
    dp, ctx = mesh.devices.shape
    fine = Mesh(mesh.devices.reshape(dp // 4, 2, 2, ctx), ("group", "pair", "core", "ctx"))
    heads = ("group", "pair", "core")
    return jax.shard_map(
        on_device,
        mesh=fine,
        in_specs=(P("ctx", heads), P("ctx", None), P("ctx", None), P("ctx", heads), P()),
        out_specs=(P("ctx", heads), P("ctx", heads), P("ctx", heads)),
        check_vma=False,
    )
```

time: 608 us -> 86.9 us (0.14)
  waiting for transfers between devices: 422 us -> 4.69 us
  matrix products: 69.1 us -> 0 us
  other arithmetic: 48 us -> 1.4 us
  blocking collectives: 0 us -> 19.7 us
  Pallas kernels: 0 us -> 13.8 us
  local copies, waits for them, and re-layouts: 22.3 us -> 10 us
  between operations: 14 us -> 4.34 us
    all_gather x2 -> x0, waiting for transfers between devices: 259 us -> none  [the longest x1 133 us: on_device(): lax.all_gather(key_own, 'ctx', axis=0, tiled=True)]
    reduce_scatter x1 -> x0, waiting for transfers between devices: 163 us -> none  [on_device(): lax.psum_scatter(lax.fori_loop(0, rows * lax.axis_size('ctx') // size, on...]
    dot_general x56 -> x0, matrix products: 69.1 us -> none  [the longest x24 29.9 us: tiles(): jnp.einsum('rngd,bnd->ngrb', query_four, key_blk, preferred_element_type=...]
    add x43 -> x0, other arithmetic: 40.2 us -> none  [the longest x32 40.1 us: on_device(): jnp.where(query_rows < half_rows, mine[0], mine[1]) * half_rows]
    all_to_all x0 -> x2, starting transfers between devices: none -> 21.2 us  [the longest x1 13.5 us: on_device(): kv = lax.all_to_all(kv_send, 'ctx', 0, 0, tiled=True)]
    all_gather x0 -> x4, blocking collectives: none -> 19.7 us  [the longest x1 7.78 us: on_device(): stats_all = lax.all_gather(stats, ('pair', 'core'), axis=0)]
    ppermute x2 -> x4, starting transfers between devices: 28.6 us -> 11 us  [the longest x3 7.87 us: on_device(): lax.ppermute(piece, ('pair', 'core'), [(i, i ^ step) for i in range(4)])]
    pallas_call x0 -> x6, Pallas kernels: none -> 13.8 us  [call(): pl.pallas_call(kernel, out_shape=out_shape, in_specs=[pl.BlockSpec(memory...]
  transfers between devices with their start and end apart: 5 -> 6, of which waited for: 3 -> 2; matrix products, arithmetic and copies ran while one was open for 11% -> 3% of each run, Pallas kernels for 0% -> 2%
where the time goes in v1:
time: 86.9 us; the launch traced here: 86.1 us
  starting transfers between devices  32.2 us (37%)
  blocking collectives  19.7 us (23%)
  Pallas kernels  13.8 us (16%)
  local copies, waits for them, and re-layouts  10 us (12%)
  waiting for transfers between devices  4.69 us (5%)
  between operations  4.34 us (5%)
  other arithmetic  1.4 us (2%)
    pallas_call x6, Pallas kernels, call(): pl.pallas_call(kernel, out_shape=out_shape, in_specs=[pl.BlockSpec(memory...  13.8 us
    all_to_all x1, starting transfers between devices, on_device(): kv = lax.all_to_all(kv_send, 'ctx', 0, 0, tiled=True)  13.5 us
    unnamed x11, local copies, waits for them, and re-layouts  8.67 us
    ppermute x3, starting transfers between devices, on_device(): lax.ppermute(piece, ('pair', 'core'), [(i, i ^ step) for i in range(4)])  7.87 us
    all_gather x1, blocking collectives, on_device(): stats_all = lax.all_gather(stats, ('pair', 'core'), axis=0)  7.78 us
    all_to_all x1, starting transfers between devices, on_device(): dkv = lax.all_to_all(dkv_send, 'ctx', 0, 0, tiled=True)  7.71 us
    all_gather x1, blocking collectives, on_device(): whole = lax.all_gather(summed, ('pair', 'core'), axis=0)  6.69 us
    ppermute x3, waiting for transfers between devices, on_device(): lax.ppermute(piece, ('pair', 'core'), [(i, i ^ step) for i in range(4)])  4.68 us
  transfers between devices with their start and end apart: 6, of which 2 were waited for; matrix products, arithmetic and copies ran while one was open for 3% of the time, Pallas kernels for 2%

profile of v1, /device:TPU:1, one launch (start us, length us, event | category | flops | bytes accessed | tf_op | source)
XLA Modules:
  0.0 86.1 jit_solution(9409336462977724188)
XLA Ops:
  0.6 0.6 pad_add_fusion.meta
  1.2 2.3 %shard_map.76 = bf16[32,64,128]{2,1,0:T(8,128)(2,1)} custom-call(s32[2]{0:T(128)} %pad_add_fusion.meta, bf16[128,512]{1,0:T(8,128)(2,1)} %keys.1, bf16[128,512]{1,0:T(8,128)(2,1)} %values.1), custom_call_target="tpu_custom_call" | custom-call | flops 1048576 | bytes 1048576 | tf_op jit(solution)/shard_map/pallas_call | solution.py:228
  3.5 13.5 %all-to-all-start = ((bf16[32,64,128]{2,1,0:T(8,128)(2,1)}), bf16[32,64,128]{2,1,0:T(8,128)(2,1)S(1)}, u32[]{:S(2)}, u32[]{:S(2)}) async-start(bf16[32,64,128]{2,1,0:T(8,128)(2,1)} %shard_map.76), calls=%async_computation | async-start | bytes 1048576 | tf_op jit(solution)/shard_map/all_to_all | solution.py:261
  17.0 0.0 copy-start
  17.0 0.9 %copy-done = bf16[128,512]{1,0:T(8,128)(2,1)S(1)} copy-done((bf16[128,512]{1,0:T(8,128)(2,1)S(1)}, bf16[128,512]{1,0:T(8,128)(2,1)}, u32[]{:S(2)}) %copy-start) | copy-done | bytes 131096
  17.9 0.0 copy-start.1
  17.9 0.9 %copy-done.1 = bf16[128,512]{1,0:T(8,128)(2,1)S(1)} copy-done((bf16[128,512]{1,0:T(8,128)(2,1)S(1)}, bf16[128,512]{1,0:T(8,128)(2,1)}, u32[]{:S(2)}) %copy-start.1) | copy-done | bytes 131096
  18.9 3.1 %collective-permute-start = (bf16[2,128,512]{2,1,0:T(8,128)(2,1)S(1)}, bf16[2,128,512]{2,1,0:T(8,128)(2,1)S(1)}, u32[]{:S(2)}, u32[]{:S(2)}) collective-permute-start(bf16[2,128,512]{2,1,0:T(8,128)(2,1)S(1)} %shard_map.77), channel_id=1, source_target_pairs={{0,64},{64,0},{1,65},{65,1},{2,66},{66,2},{3,67},{67,3},{4,68},{68... | collective-permute-start | bytes 786440 | tf_op jit(solution)/shard_map/ppermute | solution.py:263
  22.0 0.8 constant_dynamic-slice_fusion
  22.7 0.5 fusion
  26.9 0.8 copy.15.spans
  27.6 0.1 stack.36.meta
  27.7 3.0 %all-gather = bf16[4,128,512]{2,1,0:T(8,128)(2,1)S(1)} all-gather(bf16[2,128,512]{2,1,0:T(8,128)(2,1)S(1)} %shard_map.77), channel_id=2, replica_groups=mesh['group'=4,'pair'=2,'core'=2,'ctx'=32] {'core'}, dimensions={0}, use_global_device_ids=true | all-gather | bytes 786432 | tf_op jit(solution)/shard_map/all_gather | solution.py:264
  30.7 0.0 collective-permute-done
  30.7 2.2 %all-gather.1 = bf16[4,128,512]{2,1,0:T(8,128)(2,1)S(1)} all-gather(bf16[2,128,512]{2,1,0:T(8,128)(2,1)S(1)} %collective-permute-done), channel_id=3, replica_groups=mesh['group'=4,'pair'=2,'core'=2,'ctx'=32] {'core'}, dimensions={0}, use_global_device_ids=true | all-gather | bytes 786432 | tf_op jit(solution)/shard_map/all_gather | solution.py:265
  32.9 0.0 all-to-all-done.kv
  32.9 3.0 %shard_map.78 = f32[8,1024]{1,0:T(8,128)S(1)} custom-call(s32[6]{0:T(128)S(1)} %stack.36.meta, s32[32,2]{1,0:T(8,128)S(1)} %copy.15.spans, bf16[32,64,128]{2,1,0:T(8,128)(2,1)S(1)} %all-to-all-done.kv, bf16[2,2,128,512]{3,2,1,0:T(8,128)(2,1)S(1)} %bitcast.10, bf16[2,2,128,512]{3,2,1,0:T(8,128)(2,1)S(1)} %bitcast.12), custom_call_target="tpu_custom_call" | custom-call | flops 1073741824 | bytes 1048576 | tf_op jit(solution)/shard_map/pallas_call | solution.py:228
  35.9 7.8 %all-gather.2 = f32[32,1024]{1,0:T(8,128)S(1)} all-gather(f32[8,1024]{1,0:T(8,128)S(1)} %shard_map.78), channel_id=4, replica_groups=mesh['group'=4,'pair'=2,'core'=2,'ctx'=32] {'pair','core'}, dimensions={0}, use_global_device_ids=true | all-gather | bytes 163840 | tf_op jit(solution)/shard_map/all_gather | solution.py:277
  43.7 5.0 %shard_map.79 = (bf16[32,64,128]{2,1,0:T(8,128)(2,1)}, bf16[5,256,1024]{2,1,0:T(8,128)(2,1)S(1)}) custom-call(s32[6]{0:T(128)S(1)} %stack.36.meta, s32[32,2]{1,0:T(8,128)S(1)} %copy.15.spans, f32[4,8,1024]{2,1,0:T(8,128)S(1)} %bitcast.14, bf16[32,64,128]{2,1,0:T(8,128)(2,1)S(1)} %all-to-all-done.kv, bf16[2,2,128,512]{3,2,1,0:T(8,128)(2,1)S(1)} %bitcast.11, ...), custom_call_target="tpu_custom_call" | custom-call | flops 2147483648 | bytes 1048576 | tf_op jit(solution)/shard_map/pallas_call | solution.py:228
  48.7 0.0 copy-start.2
  48.7 1.5 %copy-done.2 = bf16[5,256,1024]{2,1,0:T(8,128)(2,1)} copy-done((bf16[5,256,1024]{2,1,0:T(8,128)(2,1)}, bf16[5,256,1024]{2,1,0:T(8,128)(2,1)S(1)}, u32[]{:S(2)}) %copy-start.2) | copy-done | bytes 2621464
  50.2 7.7 %all-to-all-start.1 = ((bf16[32,64,128]{2,1,0:T(8,128)(2,1)}), bf16[32,64,128]{2,1,0:T(8,128)(2,1)S(1)}, u32[]{:S(2)}, u32[]{:S(2)}) async-start(bf16[32,64,128]{2,1,0:T(8,128)(2,1)} %get-tuple-element.16), calls=%async_computation.1 | async-start | bytes 1048576 | tf_op jit(solution)/shard_map/all_to_all | solution.py:292
  57.9 0.0 copy-start.3
  57.9 1.7 %copy-done.3 = bf16[5,256,1024]{2,1,0:T(8,128)(2,1)S(1)} copy-done((bf16[5,256,1024]{2,1,0:T(8,128)(2,1)S(1)}, bf16[5,256,1024]{2,1,0:T(8,128)(2,1)}, u32[]{:S(2)}) %copy-start.3) | copy-done | bytes 2621464
  59.7 1.7 %shard_map.80 = (bf16[128,512]{1,0:T(8,128)(2,1)S(1)}, bf16[128,512]{1,0:T(8,128)(2,1)S(1)}, bf16[128,512]{1,0:T(8,128)(2,1)S(1)}, bf16[128,512]{1,0:T(8,128)(2,1)S(1)}) custom-call(s32[6]{0:T(128)S(1)} %stack.36.meta, s32[32,2]{1,0:T(8,128)S(1)} %copy.15.spans, bf16[32,64,128]{2,1,0:T(8,128)(2,1)S(1)} %all-to-all-done.kv, bf16[5,256,1024]{2,1,0:T(8,128)(2,1)S(1)} %copy-done.3), custom_call_target="tpu_custom_call" | custom-call | flops 2147483648 | bytes 1048576 | tf_op jit(solution)/shard_map/pallas_call | solution.py:228
  61.4 2.4 %collective-permute-start.1 = (bf16[128,512]{1,0:T(8,128)(2,1)S(1)}, bf16[128,512]{1,0:T(8,128)(2,1)S(1)}, u32[]{:S(2)}, u32[]{:S(2)}) collective-permute-start(bf16[128,512]{1,0:T(8,128)(2,1)S(1)} %get-tuple-element.13), channel_id=1, source_target_pairs={{0,32},{32,0},{64,96},{96,64},{1,33},{33,1},{65,97},{97,65},{2,34}... | collective-permute-start | bytes 393224 | tf_op jit(solution)/shard_map/ppermute | solution.py:308
  63.7 2.2 %collective-permute-start.2 = (bf16[128,512]{1,0:T(8,128)(2,1)S(1)}, bf16[128,512]{1,0:T(8,128)(2,1)S(1)}, u32[]{:S(2)}, u32[]{:S(2)}) collective-permute-start(bf16[128,512]{1,0:T(8,128)(2,1)S(1)} %get-tuple-element.14), channel_id=1, source_target_pairs={{0,64},{32,96},{64,0},{96,32},{1,65},{33,97},{65,1},{97,33},{2,66}... | collective-permute-start | bytes 393224 | tf_op jit(solution)/shard_map/ppermute | solution.py:308
  65.9 3.3 %collective-permute-start.3 = (bf16[128,512]{1,0:T(8,128)(2,1)S(1)}, bf16[128,512]{1,0:T(8,128)(2,1)S(1)}, u32[]{:S(2)}, u32[]{:S(2)}) collective-permute-start(bf16[128,512]{1,0:T(8,128)(2,1)S(1)} %get-tuple-element.15), channel_id=1, source_target_pairs={{0,96},{32,64},{64,32},{96,0},{1,97},{33,65},{65,33},{97,1},{2,98}... | collective-permute-start | bytes 393224 | tf_op jit(solution)/shard_map/ppermute | solution.py:308
  69.3 0.0 collective-permute-done.1
  69.3 1.4 %collective-permute-done.2 = bf16[128,512]{1,0:T(8,128)(2,1)S(1)} collective-permute-done((bf16[128,512]{1,0:T(8,128)(2,1)S(1)}, bf16[128,512]{1,0:T(8,128)(2,1)S(1)}, u32[]{:S(2)}, u32[]{:S(2)}) %collective-permute-start.2) | collective-permute-done | bytes 131104 | tf_op jit(solution)/shard_map/ppermute | solution.py:308
  70.7 3.3 %collective-permute-done.3 = bf16[128,512]{1,0:T(8,128)(2,1)S(1)} collective-permute-done((bf16[128,512]{1,0:T(8,128)(2,1)S(1)}, bf16[128,512]{1,0:T(8,128)(2,1)S(1)}, u32[]{:S(2)}, u32[]{:S(2)}) %collective-permute-start.3) | collective-permute-done | bytes 131104 | tf_op jit(solution)/shard_map/ppermute | solution.py:308
  74.0 0.7 add_convert_fusion
  74.7 0.0 all-to-all-done.1
  74.7 0.1 reduce_sum.12
  74.8 6.7 %all-gather.3 = bf16[256,128]{1,0:T(8,128)(2,1)} all-gather(bf16[64,128]{1,0:T(8,128)(2,1)S(1)} %reduce_sum.12), channel_id=5, replica_groups=mesh['group'=4,'pair'=2,'core'=2,'ctx'=32] {'pair','core'}, dimensions={0}, use_global_device_ids=true | all-gather | bytes 81920 | tf_op jit(solution)/shard_map/all_gather | solution.py:311
  81.5 1.8 %shard_map.81 = (bf16[128,32]{1,0:T(8,128)(2,1)}, bf16[128,32]{1,0:T(8,128)(2,1)}) custom-call(bf16[4,64,128]{2,1,0:T(8,128)(2,1)} %bitcast.15, s32[1]{0:T(128)} %bitcast.1.sharer), custom_call_target="tpu_custom_call" | custom-call | flops 1048576 | bytes 1048576 | tf_op jit(solution)/shard_map/pallas_call | solution.py:228
  83.2 1.4 %copy.16 = bf16[128,32]{0,1:T(8,128)(2,1)} copy(bf16[128,32]{1,0:T(8,128)(2,1)} %get-tuple-element.23) | data formatting | bytes 16384
  84.7 1.4 %copy.17 = bf16[128,32]{0,1:T(8,128)(2,1)} copy(bf16[128,32]{1,0:T(8,128)(2,1)} %get-tuple-element.24) | data formatting | bytes 16384
  (1 shorter events, 0.0 us)
Async XLA Ops:
  3.5 29.4 %all-to-all-start = ((bf16[32,64,128]{2,1,0:T(8,128)(2,1)}), bf16[32,64,128]{2,1,0:T(8,128)(2,1)S(1)}, u32[]{:S(2)}, u32[]{:S(2)}) async-start(bf16[32,64,128]{2,1,0:T(8,128)(2,1)} %shard_map.76), calls=%async_computation | async-start | bytes 1048576 | tf_op jit(solution)/shard_map/all_to_all | solution.py:261
  17.0 0.9 %copy-start = (bf16[128,512]{1,0:T(8,128)(2,1)S(1)}, bf16[128,512]{1,0:T(8,128)(2,1)}, u32[]{:S(2)}) copy-start(bf16[128,512]{1,0:T(8,128)(2,1)} %queries.1) | copy-start | bytes 393220
  17.9 0.9 %copy-start.1 = (bf16[128,512]{1,0:T(8,128)(2,1)S(1)}, bf16[128,512]{1,0:T(8,128)(2,1)}, u32[]{:S(2)}) copy-start(bf16[128,512]{1,0:T(8,128)(2,1)} %cotan.1) | copy-start | bytes 393220
  18.9 11.9 %collective-permute-start = (bf16[2,128,512]{2,1,0:T(8,128)(2,1)S(1)}, bf16[2,128,512]{2,1,0:T(8,128)(2,1)S(1)}, u32[]{:S(2)}, u32[]{:S(2)}) collective-permute-start(bf16[2,128,512]{2,1,0:T(8,128)(2,1)S(1)} %shard_map.77), channel_id=1, source_target_pairs={{0,64},{64,0},{1,65},{65,1},{2,66},{66,2},{3,67},{67,3},{4,68},{68... | collective-permute-start | bytes 786440 | tf_op jit(solution)/shard_map/ppermute | solution.py:263
  48.7 1.5 %copy-start.2 = (bf16[5,256,1024]{2,1,0:T(8,128)(2,1)}, bf16[5,256,1024]{2,1,0:T(8,128)(2,1)S(1)}, u32[]{:S(2)}) copy-start(bf16[5,256,1024]{2,1,0:T(8,128)(2,1)S(1)} %get-tuple-element.11.dscore) | copy-start | bytes 7864324
  50.2 24.5 %all-to-all-start.1 = ((bf16[32,64,128]{2,1,0:T(8,128)(2,1)}), bf16[32,64,128]{2,1,0:T(8,128)(2,1)S(1)}, u32[]{:S(2)}, u32[]{:S(2)}) async-start(bf16[32,64,128]{2,1,0:T(8,128)(2,1)} %get-tuple-element.16), calls=%async_computation.1 | async-start | bytes 1048576 | tf_op jit(solution)/shard_map/all_to_all | solution.py:292
  57.9 1.7 %copy-start.3 = (bf16[5,256,1024]{2,1,0:T(8,128)(2,1)S(1)}, bf16[5,256,1024]{2,1,0:T(8,128)(2,1)}, u32[]{:S(2)}) copy-start(bf16[5,256,1024]{2,1,0:T(8,128)(2,1)} %copy-done.2) | copy-start | bytes 7864324
  61.4 7.9 %collective-permute-start.1 = (bf16[128,512]{1,0:T(8,128)(2,1)S(1)}, bf16[128,512]{1,0:T(8,128)(2,1)S(1)}, u32[]{:S(2)}, u32[]{:S(2)}) collective-permute-start(bf16[128,512]{1,0:T(8,128)(2,1)S(1)} %get-tuple-element.13), channel_id=1, source_target_pairs={{0,32},{32,0},{64,96},{96,64},{1,33},{33,1},{65,97},{97,65},{2,34}... | collective-permute-start | bytes 393224 | tf_op jit(solution)/shard_map/ppermute | solution.py:308
  63.7 7.0 %collective-permute-start.2 = (bf16[128,512]{1,0:T(8,128)(2,1)S(1)}, bf16[128,512]{1,0:T(8,128)(2,1)S(1)}, u32[]{:S(2)}, u32[]{:S(2)}) collective-permute-start(bf16[128,512]{1,0:T(8,128)(2,1)S(1)} %get-tuple-element.14), channel_id=1, source_target_pairs={{0,64},{32,96},{64,0},{96,32},{1,65},{33,97},{65,1},{97,33},{2,66}... | collective-permute-start | bytes 393224 | tf_op jit(solution)/shard_map/ppermute | solution.py:308
  65.9 8.0 %collective-permute-start.3 = (bf16[128,512]{1,0:T(8,128)(2,1)S(1)}, bf16[128,512]{1,0:T(8,128)(2,1)S(1)}, u32[]{:S(2)}, u32[]{:S(2)}) collective-permute-start(bf16[128,512]{1,0:T(8,128)(2,1)S(1)} %get-tuple-element.15), channel_id=1, source_target_pairs={{0,96},{32,64},{64,32},{96,0},{1,97},{33,65},{65,33},{97,1},{2,98}... | collective-permute-start | bytes 393224 | tf_op jit(solution)/shard_map/ppermute | solution.py:308

commit v2 on v1

--- a/solution.py
+++ b/solution.py
@@ -30,7 +30,19 @@
     return lax.dot_general(a, b, dims, preferred_element_type=F32)
 
 
-def pick_kernel(meta, keys, values, kv_out, held, sems):
+def place(spans=None):
+    pair = lax.axis_index("pair")
+    sharer = pair * 2 + lax.axis_index("core")
+    if spans is None:
+        return lax.axis_index("group"), sharer
+    ctx = lax.axis_index("ctx")
+    first, second = spans[0, ctx], spans[1, ctx]
+    swapped = jnp.where(first > second, 1, 0)
+    return lax.axis_index("group"), sharer, jnp.minimum(first, second), jnp.maximum(first, second), pair, swapped
+
+
+def pick_kernel(keys, values, kv_out, held, sems):
+    meta = place()
     col = pl.multiple_of(meta[0] * HD, HD)
     copies = []
     for which, ref in enumerate((keys, values)):
@@ -58,7 +70,7 @@
 def load(meta, spans, kv, own, other, ks, vs, qs, gs):
     for src in range(kv.shape[0]):
         for half in range(2):
-            at = pl.multiple_of(spans[src, half] * SUB, SUB)
+            at = pl.multiple_of(spans[half, src] * SUB, SUB)
             ks[pl.ds(at, SUB), :] = kv[src, half * SUB : (half + 1) * SUB, :]
             vs[pl.ds(at, SUB), :] = kv[src, (2 + half) * SUB : (3 + half) * SUB, :]
     heads = own.shape[3] // HD
@@ -75,10 +87,10 @@
                     gs[rank, pl.ds(at, SPAN), :] = ref[core, 1, rows, cols]
 
 
-def offsets(width):
-    key = lax.broadcasted_iota(jnp.int32, (TILE, width), 0)
-    row = lax.broadcasted_iota(jnp.int32, (TILE, width), 1)
-    return (key // SUB) * SPAN + key % SUB - row % SPAN
+def offsets():
+    key = lax.broadcasted_iota(jnp.int32, (TILE, WIDTH), 0)
+    row = lax.broadcasted_iota(jnp.int32, (TILE, WIDTH), 1)
+    return (key >> 4) * SPAN + (key & (SUB - 1)) - (row & (SPAN - 1))
 
 
 def units(meta):
@@ -100,7 +112,9 @@
 WIDTH = 256
 
 
-def stats_kernel(meta, spans, kv, own, other, out, ks, vs, qs, gs, part):
+def stats_kernel(spans, kv, own, other, out, ks, vs, qs, gs, part, off):
+    meta = place(spans)
+    off[...] = offsets()
     load(meta, spans, kv, own, other, ks, vs, qs, gs)
     rows = qs.shape[1]
     for unit, (half, tile, masked) in enumerate(units(meta)):
@@ -111,7 +125,7 @@
             cols = slice(first, first + WIDTH)
             score = dot(key, qs[half, cols, :], NT)
             if masked:
-                score = jnp.where(offsets(WIDTH) <= bound(meta, half, tile), score, LOW)
+                score = jnp.where(off[...] <= bound(meta, half, tile), score, LOW)
             top = jnp.maximum(jnp.max(score, axis=0, keepdims=True), FLOOR)
             weight = jnp.exp2((score - top) * EXP2)
             dprob = dot(value, gs[half, cols, :], NT)
@@ -137,18 +151,14 @@
     out[6:8, :] = jnp.zeros((2, rows), F32)
 
 
-def sort_keys(spans, kv, first, out):
-    for src in range(kv.shape[0]):
-        for half in range(2):
-            at = pl.multiple_of(spans[src, half] * SUB, SUB)
-            out[pl.ds(at, SUB), :] = kv[src, (first + half) * SUB : (first + half + 1) * SUB, :]
-
-
-def key_grads_kernel(
-    meta, spans, stats, kv, own, other, dkv_out, dscore_out,
-    ks, vs, qs, gs, row_stats, probs_b, dk, dv,
+def grads_kernel(
+    spans, stats, kv, own, other, dkv_out, dq_0, dq_1, dq_2, dq_3,
+    ks, vs, qs, gs, row_stats, probs_b, dscore_b, dk, dv, dq, kt, back, off,
 ):
+    meta = place(spans)
+    off[...] = offsets()
     load(meta, spans, kv, own, other, ks, vs, qs, gs)
+    kt[...] = ks[...].T
     rows = qs.shape[1]
     for half in range(2):
         tops = [stats[src, half * 3 : half * 3 + 1, :] for src in range(4)]
@@ -169,14 +179,15 @@
             cols = slice(first, first + WIDTH)
             score = dot(key, qs[half, cols, :], NT)
             if masked:
-                score = jnp.where(offsets(WIDTH) <= bound(meta, half, tile), score, LOW)
+                score = jnp.where(off[...] <= bound(meta, half, tile), score, LOW)
             prob = jnp.exp2((score - row_stats[half, 0:1, cols]) * EXP2) * row_stats[half, 1:2, cols]
             dprob = dot(value, gs[half, cols, :], NT)
             dscore = prob * (dprob - row_stats[half, 2:3, cols])
             probs_b[unit % 2, :, cols] = prob.astype(BF16)
-            dscore_out[unit, :, cols] = dscore.astype(BF16)
+            dscore_b[unit % 2, :, cols] = dscore.astype(BF16)
         dv_tile = dot(probs_b[unit % 2], gs[half])
-        dk_tile = dot(dscore_out[unit], qs[half])
+        dk_tile = dot(dscore_b[unit % 2], qs[half])
+        dq_half = dot(kt[:, pl.ds(at, TILE)], dscore_b[unit % 2])
         keys_of = pl.ds(at, TILE)
         if unit in (0, 2, 3):
             dv[keys_of, :] = dv_tile
@@ -184,52 +195,42 @@
         else:
             dv[keys_of, :] += dv_tile
             dk[keys_of, :] += dk_tile
-    for dest in range(dkv_out.shape[0]):
-        for half in range(2):
-            at = pl.multiple_of(spans[dest, half] * SUB, SUB)
-            dkv_out[dest, half * SUB : (half + 1) * SUB, :] = (dk[pl.ds(at, SUB), :] * SCALE).astype(BF16)
-            dkv_out[dest, (2 + half) * SUB : (3 + half) * SUB, :] = dv[pl.ds(at, SUB), :].astype(BF16)
-
-
-def query_grads_kernel(meta, spans, kv, dscore, out_0, out_1, out_2, out_3, ks, kt, dq, back):
-    sort_keys(spans, kv, 0, ks)
-    kt[...] = ks[...].T
-    for unit, (half, tile, _) in enumerate(units(meta)):
-        at = pl.multiple_of(tile * TILE, TILE) if unit == 4 else tile * TILE
-        dq_half = dot(kt[:, pl.ds(at, TILE)], dscore[unit])
         if unit in (0, 1):
             dq[half] = dq_half
         else:
             dq[half] += dq_half
-    heads = out_0.shape[1] // HD
+    for dest in range(dkv_out.shape[0]):
+        for half in range(2):
+            at = pl.multiple_of(spans[half, dest] * SUB, SUB)
+            dkv_out[dest, half * SUB : (half + 1) * SUB, :] = (dk[pl.ds(at, SUB), :] * SCALE).astype(BF16)
+            dkv_out[dest, (2 + half) * SUB : (3 + half) * SUB, :] = dv[pl.ds(at, SUB), :].astype(BF16)
+    heads = dq_0.shape[1] // HD
     for half in range(2):
         back[...] = (dq[half ^ meta[5]] * SCALE).T.astype(BF16)
-        for step, out in enumerate((out_0, out_1, out_2, out_3)):
+        for step, out in enumerate((dq_0, dq_1, dq_2, dq_3)):
             for head in range(heads):
                 at = pl.multiple_of(((meta[1] ^ step) * heads + head) * SPAN, SPAN)
                 out[half * SPAN : (half + 1) * SPAN, head * HD : (head + 1) * HD] = back[pl.ds(at, SPAN), :]
 
 
-def split_kernel(whole, sharer, grad_keys, grad_values):
-    wide = grad_keys.shape[1]
+def split_kernel(whole, grad_keys, grad_values, turned):
+    _, sharer = place()
+    wide = grad_keys.shape[0]
     for which, out in enumerate((grad_keys, grad_values)):
+        pieces = []
         for half in range(2):
-            for src in range(4):
-                at = (which * 2 + half) * SUB
-                block = whole[src, at : at + SUB, :]
-                part = block[:, 3 * wide :]
-                for mine in range(3):
-                    part = jnp.where(sharer[0] == mine, block[:, mine * wide : (mine + 1) * wide], part)
-                row = half * SPAN + src * SUB
-                out[row : row + SUB, :] = part
-
-
-def call(kernel, out_shape, scratch, flops, spaces, *args, limit=32):
+            at = (which * 2 + half) * SUB
+            pieces += [whole[src, at : at + SUB, :] for src in range(4)]
+        turned[...] = jnp.concatenate(pieces, axis=0).astype(F32).T
+        out[...] = turned[pl.ds(pl.multiple_of(sharer * wide, wide), wide), :].astype(BF16)
+
+
+def call(kernel, out_shape, scratch, flops, spaces, *args, limit=32, outs=None):
     return pl.pallas_call(
         kernel,
         out_shape=out_shape,
         in_specs=[pl.BlockSpec(memory_space={"s": pltpu.SMEM, "v": VM, "a": pl.ANY}[space]) for space in spaces],
-        out_specs=jax.tree.map(lambda _: pl.BlockSpec(memory_space=VM), out_shape),
+        out_specs=outs or jax.tree.map(lambda _: pl.BlockSpec(memory_space=VM), out_shape),
         scratch_shapes=scratch,
         cost_estimate=pl.CostEstimate(flops=flops, bytes_accessed=1 << 20, transcendentals=0),
         compiler_params=pltpu.CompilerParams(vmem_limit_bytes=limit << 20),
@@ -239,14 +240,7 @@
 def on_device(queries, keys, values, grad_out, spans):
     rows, width = queries.shape
     ctx_count = lax.axis_size("ctx")
-    group_index = lax.axis_index("group")
-    x_index = lax.axis_index("pair")
-    sharer = x_index * 2 + lax.axis_index("core")
-    ctx_index = lax.axis_index("ctx")
-    mine = lax.dynamic_slice_in_dim(spans, ctx_index, 1, 0).reshape(2)
-    low, high = jnp.minimum(mine[0], mine[1]), jnp.maximum(mine[0], mine[1])
-    meta = jnp.stack((group_index, sharer, low, high, x_index, mine[0] > mine[1])).astype(jnp.int32)
-    pick_meta = jnp.stack((group_index, sharer)).astype(jnp.int32)
+    spans = spans.T
     sds = jax.ShapeDtypeStruct
     blocks = sds((ctx_count, 4 * SUB, HD), BF16)
     kv_send = call(
@@ -254,8 +248,8 @@
         blocks,
         [VM((4 * SUB, HD), BF16), pltpu.SemaphoreType.DMA((4,))],
         1 << 20,
-        "saa",
-        pick_meta, keys, values,
+        "aa",
+        keys, values,
         limit=60,
     )
     kv = lax.all_to_all(kv_send, "ctx", 0, 0, tiled=True)
@@ -266,52 +260,45 @@
     stacked = 2 * 2 * (width // HD) * SPAN
     keys_held = 2 * ctx_count * SUB
     common = [VM((keys_held, HD), BF16)] * 2 + [VM((2, stacked, HD), BF16)] * 2
+    mask = VM((TILE, WIDTH), jnp.int32)
     stats = call(
         stats_kernel,
         sds((8, stacked), F32),
-        common + [VM((5, 8, stacked), F32)],
+        common + [VM((5, 8, stacked), F32), mask],
         1 << 30,
-        "ssvvv",
-        meta, spans, kv, own, other,
+        "svvv",
+        spans, kv, own, other,
     )
     stats_all = lax.all_gather(stats, ("pair", "core"), axis=0)
-    dkv_send, dscore = call(
-        key_grads_kernel,
-        (blocks, sds((5, TILE, stacked), BF16)),
+    dkv_send, dq_mine, *dq_send = call(
+        grads_kernel,
+        (blocks,) + (sds((rows, width), BF16),) * 4,
         common
         + [
             VM((2, 8, stacked), F32),
             VM((2, TILE, stacked), BF16),
+            VM((2, TILE, stacked), BF16),
             VM((keys_held, HD), F32),
             VM((keys_held, HD), F32),
+            VM((2, HD, stacked), F32),
+            VM((HD, keys_held), BF16),
+            VM((stacked, HD), BF16),
+            mask,
         ],
         1 << 31,
-        "ssvvvv",
-        meta, spans, stats_all, kv, own, other,
+        "svvvv",
+        spans, stats_all, kv, own, other,
     )
     dkv = lax.all_to_all(dkv_send, "ctx", 0, 0, tiled=True)
-    dq_mine, *dq_send = call(
-        query_grads_kernel,
-        (sds((rows, width), BF16),) * 4,
-        [
-            VM((keys_held, HD), BF16),
-            VM((HD, keys_held), BF16),
-            VM((2, HD, stacked), F32),
-            VM((stacked, HD), BF16),
-        ],
-        1 << 31,
-        "ssvv",
-        meta, spans, kv, dscore,
-    )
     grad_queries = dq_mine.astype(F32)
     for step, piece in enumerate(dq_send, 1):
         grad_queries += lax.ppermute(piece, ("pair", "core"), [(i, i ^ step) for i in range(4)]).astype(F32)
     grad_queries = grad_queries.astype(BF16)
     summed = jnp.sum(dkv.astype(F32), axis=0).astype(BF16)
     whole = lax.all_gather(summed, ("pair", "core"), axis=0)
-    part = sds((rows, HD // 4), BF16)
-    grad_keys, grad_values = call(split_kernel, (part, part), [], 1 << 20, "vs", whole, sharer.reshape(1), limit=60)
-    return (grad_queries, grad_keys, grad_values)
+    part = sds((HD // 4, rows), BF16)
+    grad_keys, grad_values = call(split_kernel, (part, part), [VM((HD, rows), F32)], 1 << 20, "v", whole, limit=60)
+    return (grad_queries, grad_keys.T, grad_values.T)
 
 
 def solution(mesh):

time: 86.9 us -> 78.7 us (0.906)
  local copies, waits for them, and re-layouts: 10 us -> 0.69 us
  waiting for transfers between devices: 4.69 us -> 12.1 us
  between operations: 4.34 us -> 0.75 us
  blocking collectives: 19.7 us -> 23.2 us
  starting transfers between devices: 32.2 us -> 29 us
  Pallas kernels: 13.8 us -> 11.6 us
    unnamed x11 -> x6, local copies, waits for them, and re-layouts: 8.67 us -> 0.69 us
    all_to_all x1, starting transfers between devices: 7.71 us -> 4.43 us  [on_device(): dkv = lax.all_to_all(dkv_send, 'ctx', 0, 0, tiled=True)]
    ppermute x1, waiting for transfers between devices: 0.01 us -> 2.58 us  [on_device(): crossed = lax.ppermute(qd, 'pair', [(0, 1), (1, 0)])]
    all_to_all x1, waiting for transfers between devices: 0.01 us -> 2.44 us  [on_device(): kv = lax.all_to_all(kv_send, 'ctx', 0, 0, tiled=True)]
    pallas_call x6 -> x5, Pallas kernels: 13.8 us -> 11.6 us  [call(): pl.pallas_call(kernel, out_shape=out_shape, in_specs=[pl.BlockSpec(memory...]
    all_to_all x1, waiting for transfers between devices: 0.01 us -> 1.83 us  [on_device(): dkv = lax.all_to_all(dkv_send, 'ctx', 0, 0, tiled=True)]
    all_gather x1, blocking collectives: 2.17 us -> 3.66 us  [on_device(): other = lax.all_gather(crossed, 'core', axis=0)]
    all_gather x1, blocking collectives: 6.69 us -> 7.75 us  [on_device(): whole = lax.all_gather(summed, ('pair', 'core'), axis=0)]
  transfers between devices with their start and end apart: 6 -> 6, of which waited for: 2 -> 5; matrix products, arithmetic and copies ran while one was open for 3% -> 1% of each run, Pallas kernels for 2% -> 0%
where the time goes in v2:
time: 78.7 us; the launch traced here: 78.2 us
  starting transfers between devices  29 us (37%)
  blocking collectives  23.2 us (29%)
  waiting for transfers between devices  12.1 us (15%)
  Pallas kernels  11.6 us (15%)
  other arithmetic  0.81 us (1%)
    all_to_all x1, starting transfers between devices, on_device(): kv = lax.all_to_all(kv_send, 'ctx', 0, 0, tiled=True)  13.6 us
    pallas_call x5, Pallas kernels, call(): pl.pallas_call(kernel, out_shape=out_shape, in_specs=[pl.BlockSpec(memory...  11.6 us
    all_gather x1, blocking collectives, on_device(): stats_all = lax.all_gather(stats, ('pair', 'core'), axis=0)  8.76 us
    ppermute x3, starting transfers between devices, on_device(): lax.ppermute(piece, ('pair', 'core'), [(i, i ^ step) for i in range(4)])  7.87 us
    all_gather x1, blocking collectives, on_device(): whole = lax.all_gather(summed, ('pair', 'core'), axis=0)  7.75 us
    ppermute x3, waiting for transfers between devices, on_device(): lax.ppermute(piece, ('pair', 'core'), [(i, i ^ step) for i in range(4)])  5.25 us
    all_to_all x1, starting transfers between devices, on_device(): dkv = lax.all_to_all(dkv_send, 'ctx', 0, 0, tiled=True)  4.43 us
    all_gather x1, blocking collectives, on_device(): other = lax.all_gather(crossed, 'core', axis=0)  3.66 us
  transfers between devices with their start and end apart: 6, of which 5 were waited for; matrix products, arithmetic and copies ran while one was open for 1% of the time, Pallas kernels for 0%

profile of v2, /device:TPU:1, one launch (start us, length us, event | category | flops | bytes accessed | tf_op | source)
XLA Modules:
  0.0 78.2 jit_solution(13755265065188308705)
XLA Ops:
  0.6 1.6 %shard_map.76 = bf16[32,64,128]{2,1,0:T(8,128)(2,1)} custom-call(bf16[128,512]{1,0:T(8,128)(2,1)} %keys.1, bf16[128,512]{1,0:T(8,128)(2,1)} %values.1), custom_call_target="tpu_custom_call" | custom-call | flops 1048576 | bytes 1048576 | tf_op jit(solution)/shard_map/pallas_call | solution.py:229
  2.3 0.0 copy-start
  2.3 0.0 copy-start.1
  2.3 13.6 %all-to-all-start = ((bf16[32,64,128]{2,1,0:T(8,128)(2,1)}), bf16[32,64,128]{2,1,0:T(8,128)(2,1)S(1)}, u32[]{:S(2)}, u32[]{:S(2)}) async-start(bf16[32,64,128]{2,1,0:T(8,128)(2,1)} %shard_map.76), calls=%async_computation | async-start | bytes 1048576 | tf_op jit(solution)/shard_map/all_to_all | solution.py:255
  15.9 0.0 copy-done
  15.9 0.0 copy-done.1
  16.0 3.1 %collective-permute-start = (bf16[2,128,512]{2,1,0:T(8,128)(2,1)S(1)}, bf16[2,128,512]{2,1,0:T(8,128)(2,1)S(1)}, u32[]{:S(2)}, u32[]{:S(2)}) collective-permute-start(bf16[2,128,512]{2,1,0:T(8,128)(2,1)S(1)} %shard_map.77), channel_id=1, source_target_pairs={{0,64},{64,0},{1,65},{65,1},{2,66},{66,2},{3,67},{67,3},{4,68},{68... | collective-permute-start | bytes 786440 | tf_op jit(solution)/shard_map/ppermute | solution.py:257
  19.1 3.0 %all-gather = bf16[4,128,512]{2,1,0:T(8,128)(2,1)S(1)} all-gather(bf16[2,128,512]{2,1,0:T(8,128)(2,1)S(1)} %shard_map.77), channel_id=2, replica_groups=mesh['group'=4,'pair'=2,'core'=2,'ctx'=32] {'core'}, dimensions={0}, use_global_device_ids=true | all-gather | bytes 786432 | tf_op jit(solution)/shard_map/all_gather | solution.py:258
  22.1 2.6 %collective-permute-done = bf16[2,128,512]{2,1,0:T(8,128)(2,1)S(1)} collective-permute-done((bf16[2,128,512]{2,1,0:T(8,128)(2,1)S(1)}, bf16[2,128,512]{2,1,0:T(8,128)(2,1)S(1)}, u32[]{:S(2)}, u32[]{:S(2)}) %collective-permute-start) | collective-permute-done | bytes 262176 | tf_op jit(solution)/shard_map/ppermute | solution.py:257
  24.7 3.7 %all-gather.1 = bf16[4,128,512]{2,1,0:T(8,128)(2,1)S(1)} all-gather(bf16[2,128,512]{2,1,0:T(8,128)(2,1)S(1)} %collective-permute-done), channel_id=3, replica_groups=mesh['group'=4,'pair'=2,'core'=2,'ctx'=32] {'core'}, dimensions={0}, use_global_device_ids=true | all-gather | bytes 786432 | tf_op jit(solution)/shard_map/all_gather | solution.py:259
  28.4 2.4 %all-to-all-done.kv = bf16[32,64,128]{2,1,0:T(8,128)(2,1)S(1)} async-done(((bf16[32,64,128]{2,1,0:T(8,128)(2,1)}), bf16[32,64,128]{2,1,0:T(8,128)(2,1)S(1)}, u32[]{:S(2)}, u32[]{:S(2)}) %all-to-all-start) | async-done | bytes 524320 | tf_op jit(solution)/shard_map/all_to_all | solution.py:255
  30.8 0.0 copy-start.2
  30.8 0.7 copy-done.2
  31.5 2.7 %shard_map.78 = f32[8,1024]{1,0:T(8,128)S(1)} custom-call(s32[2,32]{1,0:T(2,128)S(1)} %bitcast.12, bf16[32,64,128]{2,1,0:T(8,128)(2,1)S(1)} %all-to-all-done.kv, bf16[2,2,128,512]{3,2,1,0:T(8,128)(2,1)S(1)} %bitcast.7, bf16[2,2,128,512]{3,2,1,0:T(8,128)(2,1)S(1)} %bitcast.9), custom_call_target="tpu_custom_call" | custom-call | flops 1073741824 | bytes 1048576 | tf_op jit(solution)/shard_map/pallas_call | solution.py:229
  34.2 8.8 %all-gather.2 = f32[32,1024]{1,0:T(8,128)S(1)} all-gather(f32[8,1024]{1,0:T(8,128)S(1)} %shard_map.78), channel_id=4, replica_groups=mesh['group'=4,'pair'=2,'core'=2,'ctx'=32] {'pair','core'}, dimensions={0}, use_global_device_ids=true | all-gather | bytes 163840 | tf_op jit(solution)/shard_map/all_gather | solution.py:272
  43.0 5.6 %shard_map.79 = (bf16[32,64,128]{2,1,0:T(8,128)(2,1)}, bf16[128,512]{1,0:T(8,128)(2,1)S(1)}, bf16[128,512]{1,0:T(8,128)(2,1)S(1)}, bf16[128,512]{1,0:T(8,128)(2,1)S(1)}, bf16[128,512]{1,0:T(8,128)(2,1)S(1)}) custom-call(s32[2,32]{1,0:T(2,128)S(1)} %bitcast.13, f32[4,8,1024]{2,1,0:T(8,128)S(1)} %bitcast.11, bf16[32,64,128]{2,1,0:T(8,128)(2,1)S(1)} %all-to-all-done.kv, ...), custom_call_target="tpu_custom_call" | custom-call | flops 2147483648 | bytes 1048576 | tf_op jit(solution)/shard_map/pallas_call | solution.py:229
  48.6 4.4 %all-to-all-start.1 = ((bf16[32,64,128]{2,1,0:T(8,128)(2,1)}), bf16[32,64,128]{2,1,0:T(8,128)(2,1)S(1)}, u32[]{:S(2)}, u32[]{:S(2)}) async-start(bf16[32,64,128]{2,1,0:T(8,128)(2,1)} %get-tuple-element.14), calls=%async_computation.1 | async-start | bytes 1048576 | tf_op jit(solution)/shard_map/all_to_all | solution.py:292
  53.1 2.4 %collective-permute-start.1 = (bf16[128,512]{1,0:T(8,128)(2,1)S(1)}, bf16[128,512]{1,0:T(8,128)(2,1)S(1)}, u32[]{:S(2)}, u32[]{:S(2)}) collective-permute-start(bf16[128,512]{1,0:T(8,128)(2,1)S(1)} %get-tuple-element.11), channel_id=1, source_target_pairs={{0,32},{32,0},{64,96},{96,64},{1,33},{33,1},{65,97},{97,65},{2,34}... | collective-permute-start | bytes 393224 | tf_op jit(solution)/shard_map/ppermute | solution.py:295
  55.4 3.1 %collective-permute-start.2 = (bf16[128,512]{1,0:T(8,128)(2,1)S(1)}, bf16[128,512]{1,0:T(8,128)(2,1)S(1)}, u32[]{:S(2)}, u32[]{:S(2)}) collective-permute-start(bf16[128,512]{1,0:T(8,128)(2,1)S(1)} %get-tuple-element.12), channel_id=1, source_target_pairs={{0,64},{32,96},{64,0},{96,32},{1,65},{33,97},{65,1},{97,33},{2,66}... | collective-permute-start | bytes 393224 | tf_op jit(solution)/shard_map/ppermute | solution.py:295
  58.6 2.4 %collective-permute-start.3 = (bf16[128,512]{1,0:T(8,128)(2,1)S(1)}, bf16[128,512]{1,0:T(8,128)(2,1)S(1)}, u32[]{:S(2)}, u32[]{:S(2)}) collective-permute-start(bf16[128,512]{1,0:T(8,128)(2,1)S(1)} %get-tuple-element.13), channel_id=1, source_target_pairs={{0,96},{32,64},{64,32},{96,0},{1,97},{33,65},{65,33},{97,1},{2,98}... | collective-permute-start | bytes 393224 | tf_op jit(solution)/shard_map/ppermute | solution.py:295
  61.0 0.0 collective-permute-done.1
  61.0 1.4 %collective-permute-done.2 = bf16[128,512]{1,0:T(8,128)(2,1)S(1)} collective-permute-done((bf16[128,512]{1,0:T(8,128)(2,1)S(1)}, bf16[128,512]{1,0:T(8,128)(2,1)S(1)}, u32[]{:S(2)}, u32[]{:S(2)}) %collective-permute-start.2) | collective-permute-done | bytes 131104 | tf_op jit(solution)/shard_map/ppermute | solution.py:295
  62.4 3.8 %collective-permute-done.3 = bf16[128,512]{1,0:T(8,128)(2,1)S(1)} collective-permute-done((bf16[128,512]{1,0:T(8,128)(2,1)S(1)}, bf16[128,512]{1,0:T(8,128)(2,1)S(1)}, u32[]{:S(2)}, u32[]{:S(2)}) %collective-permute-start.3) | collective-permute-done | bytes 131104 | tf_op jit(solution)/shard_map/ppermute | solution.py:295
  66.2 0.7 add_convert_fusion
  66.9 1.8 %all-to-all-done.1 = bf16[32,64,128]{2,1,0:T(8,128)(2,1)S(1)} async-done(((bf16[32,64,128]{2,1,0:T(8,128)(2,1)}), bf16[32,64,128]{2,1,0:T(8,128)(2,1)S(1)}, u32[]{:S(2)}, u32[]{:S(2)}) %all-to-all-start.1) | async-done | bytes 524320 | tf_op jit(solution)/shard_map/all_to_all | solution.py:292
  68.8 0.1 reduce_sum.12
  68.9 7.8 %all-gather.3 = bf16[256,128]{1,0:T(8,128)(2,1)} all-gather(bf16[64,128]{1,0:T(8,128)(2,1)S(1)} %reduce_sum.12), channel_id=5, replica_groups=mesh['group'=4,'pair'=2,'core'=2,'ctx'=32] {'pair','core'}, dimensions={0}, use_global_device_ids=true | all-gather | bytes 81920 | tf_op jit(solution)/shard_map/all_gather | solution.py:298
  76.6 1.6 %shard_map.80 = (bf16[32,128]{1,0:T(8,128)(2,1)}, bf16[32,128]{1,0:T(8,128)(2,1)}) custom-call(bf16[4,64,128]{2,1,0:T(8,128)(2,1)} %bitcast.14), custom_call_target="tpu_custom_call" | custom-call | flops 1048576 | bytes 1048576 | tf_op jit(solution)/shard_map/pallas_call | solution.py:229
  (1 shorter events, 0.0 us)
Async XLA Ops:
  2.3 13.6 %copy-start = (bf16[128,512]{1,0:T(8,128)(2,1)S(1)}, bf16[128,512]{1,0:T(8,128)(2,1)}, u32[]{:S(2)}) copy-start(bf16[128,512]{1,0:T(8,128)(2,1)} %queries.1) | copy-start | bytes 393220
  2.3 13.6 %copy-start.1 = (bf16[128,512]{1,0:T(8,128)(2,1)S(1)}, bf16[128,512]{1,0:T(8,128)(2,1)}, u32[]{:S(2)}) copy-start(bf16[128,512]{1,0:T(8,128)(2,1)} %cotan.1) | copy-start | bytes 393220
  2.3 28.5 %all-to-all-start = ((bf16[32,64,128]{2,1,0:T(8,128)(2,1)}), bf16[32,64,128]{2,1,0:T(8,128)(2,1)S(1)}, u32[]{:S(2)}, u32[]{:S(2)}) async-start(bf16[32,64,128]{2,1,0:T(8,128)(2,1)} %shard_map.76), calls=%async_computation | async-start | bytes 1048576 | tf_op jit(solution)/shard_map/all_to_all | solution.py:255
  16.0 8.8 %collective-permute-start = (bf16[2,128,512]{2,1,0:T(8,128)(2,1)S(1)}, bf16[2,128,512]{2,1,0:T(8,128)(2,1)S(1)}, u32[]{:S(2)}, u32[]{:S(2)}) collective-permute-start(bf16[2,128,512]{2,1,0:T(8,128)(2,1)S(1)} %shard_map.77), channel_id=1, source_target_pairs={{0,64},{64,0},{1,65},{65,1},{2,66},{66,2},{3,67},{67,3},{4,68},{68... | collective-permute-start | bytes 786440 | tf_op jit(solution)/shard_map/ppermute | solution.py:257
  30.8 0.7 copy-start.2
  48.6 20.1 %all-to-all-start.1 = ((bf16[32,64,128]{2,1,0:T(8,128)(2,1)}), bf16[32,64,128]{2,1,0:T(8,128)(2,1)S(1)}, u32[]{:S(2)}, u32[]{:S(2)}) async-start(bf16[32,64,128]{2,1,0:T(8,128)(2,1)} %get-tuple-element.14), calls=%async_computation.1 | async-start | bytes 1048576 | tf_op jit(solution)/shard_map/all_to_all | solution.py:292
  53.1 7.9 %collective-permute-start.1 = (bf16[128,512]{1,0:T(8,128)(2,1)S(1)}, bf16[128,512]{1,0:T(8,128)(2,1)S(1)}, u32[]{:S(2)}, u32[]{:S(2)}) collective-permute-start(bf16[128,512]{1,0:T(8,128)(2,1)S(1)} %get-tuple-element.11), channel_id=1, source_target_pairs={{0,32},{32,0},{64,96},{96,64},{1,33},{33,1},{65,97},{97,65},{2,34}... | collective-permute-start | bytes 393224 | tf_op jit(solution)/shard_map/ppermute | solution.py:295
  55.4 7.0 %collective-permute-start.2 = (bf16[128,512]{1,0:T(8,128)(2,1)S(1)}, bf16[128,512]{1,0:T(8,128)(2,1)S(1)}, u32[]{:S(2)}, u32[]{:S(2)}) collective-permute-start(bf16[128,512]{1,0:T(8,128)(2,1)S(1)} %get-tuple-element.12), channel_id=1, source_target_pairs={{0,64},{32,96},{64,0},{96,32},{1,65},{33,97},{65,1},{97,33},{2,66}... | collective-permute-start | bytes 393224 | tf_op jit(solution)/shard_map/ppermute | solution.py:295
  58.6 7.6 %collective-permute-start.3 = (bf16[128,512]{1,0:T(8,128)(2,1)S(1)}, bf16[128,512]{1,0:T(8,128)(2,1)S(1)}, u32[]{:S(2)}, u32[]{:S(2)}) collective-permute-start(bf16[128,512]{1,0:T(8,128)(2,1)S(1)} %get-tuple-element.13), channel_id=1, source_target_pairs={{0,96},{32,64},{64,32},{96,0},{1,97},{33,65},{65,33},{97,1},{2,98}... | collective-permute-start | bytes 393224 | tf_op jit(solution)/shard_map/ppermute | solution.py:295

commit v3 on v2

--- a/solution.py
+++ b/solution.py
@@ -62,7 +62,8 @@
         kv_out[dest] = held[...]
 
 
-def pair_kernel(queries, cotan, out):
+def pair_kernel(queries, cotan, spans, out, spans_out):
+    spans_out[...] = spans[...]
     out[0] = queries[...]
     out[1] = cotan[...]
 
@@ -253,7 +254,14 @@
         limit=60,
     )
     kv = lax.all_to_all(kv_send, "ctx", 0, 0, tiled=True)
-    qd = call(pair_kernel, sds((2, rows, width), BF16), [], 1 << 20, "vv", queries, grad_out)
+    qd, spans = call(
+        pair_kernel,
+        (sds((2, rows, width), BF16), sds(spans.shape, jnp.int32)),
+        [],
+        1 << 20,
+        "vvv",
+        queries, grad_out, spans,
+    )
     crossed = lax.ppermute(qd, "pair", [(0, 1), (1, 0)])
     own = lax.all_gather(qd, "core", axis=0)
     other = lax.all_gather(crossed, "core", axis=0)
@@ -297,7 +305,7 @@
     summed = jnp.sum(dkv.astype(F32), axis=0).astype(BF16)
     whole = lax.all_gather(summed, ("pair", "core"), axis=0)
     part = sds((HD // 4, rows), BF16)
-    grad_keys, grad_values = call(split_kernel, (part, part), [VM((HD, rows), F32)], 1 << 20, "v", whole, limit=60)
+    grad_keys, grad_values = call(split_kernel, (part, part), [VM((HD, rows), F32)], 1 << 20, "v", whole)
     return (grad_queries, grad_keys.T, grad_values.T)
 
 

time: 78.7 us -> 76.9 us (0.977)
  Pallas kernels: 11.6 us -> 10.7 us
    pallas_call x5, Pallas kernels: 11.6 us -> 10.7 us  [call(): pl.pallas_call(kernel, out_shape=out_shape, in_specs=[pl.BlockSpec(memory...]
where the time goes in v3:
time: 76.9 us; the launch traced here: 76.4 us
  starting transfers between devices  29.3 us (38%)
  blocking collectives  22.8 us (30%)
  waiting for transfers between devices  11.4 us (15%)
  Pallas kernels  10.7 us (14%)
  other arithmetic  0.81 us (1%)
    all_to_all x1, starting transfers between devices, on_device(): kv = lax.all_to_all(kv_send, 'ctx', 0, 0, tiled=True)  13.6 us
    pallas_call x5, Pallas kernels, call(): pl.pallas_call(kernel, out_shape=out_shape, in_specs=[pl.BlockSpec(memory...  10.7 us
    all_gather x1, blocking collectives, on_device(): stats_all = lax.all_gather(stats, ('pair', 'core'), axis=0)  8.77 us
    ppermute x3, starting transfers between devices, on_device(): lax.ppermute(piece, ('pair', 'core'), [(i, i ^ step) for i in range(4)])  7.87 us
    all_gather x1, blocking collectives, on_device(): whole = lax.all_gather(summed, ('pair', 'core'), axis=0)  7.31 us
    ppermute x3, waiting for transfers between devices, on_device(): lax.ppermute(piece, ('pair', 'core'), [(i, i ^ step) for i in range(4)])  5.25 us
    all_to_all x1, starting transfers between devices, on_device(): dkv = lax.all_to_all(dkv_send, 'ctx', 0, 0, tiled=True)  4.66 us
    all_gather x1, blocking collectives, on_device(): other = lax.all_gather(crossed, 'core', axis=0)  3.66 us
  transfers between devices with their start and end apart: 6, of which 5 were waited for; matrix products, arithmetic and copies ran while one was open for 1% of the time, Pallas kernels for 0%

profile of v3, /device:TPU:1, one launch (start us, length us, event | category | flops | bytes accessed | tf_op | source)
XLA Modules:
  0.0 76.4 jit_solution(11028665855163208374)
XLA Ops:
  0.6 1.6 %shard_map.77 = bf16[32,64,128]{2,1,0:T(8,128)(2,1)} custom-call(bf16[128,512]{1,0:T(8,128)(2,1)} %keys.1, bf16[128,512]{1,0:T(8,128)(2,1)} %values.1), custom_call_target="tpu_custom_call" | custom-call | flops 1048576 | bytes 1048576 | tf_op jit(solution)/shard_map/pallas_call | solution.py:230
  2.3 0.0 copy-start
  2.3 0.0 copy-start.1
  2.3 13.6 %all-to-all-start = ((bf16[32,64,128]{2,1,0:T(8,128)(2,1)}), bf16[32,64,128]{2,1,0:T(8,128)(2,1)S(1)}, u32[]{:S(2)}, u32[]{:S(2)}) async-start(bf16[32,64,128]{2,1,0:T(8,128)(2,1)} %shard_map.77), calls=%async_computation | async-start | bytes 1048576 | tf_op jit(solution)/shard_map/all_to_all | solution.py:256
  15.9 0.0 copy-start.2
  15.9 0.0 copy-done
  15.9 0.0 copy-done.1
  16.0 0.7 copy-done.2
  16.6 3.1 %collective-permute-start = (bf16[2,128,512]{2,1,0:T(8,128)(2,1)S(1)}, bf16[2,128,512]{2,1,0:T(8,128)(2,1)S(1)}, u32[]{:S(2)}, u32[]{:S(2)}) collective-permute-start(bf16[2,128,512]{2,1,0:T(8,128)(2,1)S(1)} %get-tuple-element.13), channel_id=1, source_target_pairs={{0,64},{64,0},{1,65},{65,1},{2,66},{66,2},{3,67},{67,3},{4,68},{68... | collective-permute-start | bytes 786440 | tf_op jit(solution)/shard_map/ppermute | solution.py:265
  19.8 3.0 %all-gather = bf16[4,128,512]{2,1,0:T(8,128)(2,1)S(1)} all-gather(bf16[2,128,512]{2,1,0:T(8,128)(2,1)S(1)} %get-tuple-element.13), channel_id=2, replica_groups=mesh['group'=4,'pair'=2,'core'=2,'ctx'=32] {'core'}, dimensions={0}, use_global_device_ids=true | all-gather | bytes 786432 | tf_op jit(solution)/shard_map/all_gather | solution.py:266
  22.8 2.6 %collective-permute-done = bf16[2,128,512]{2,1,0:T(8,128)(2,1)S(1)} collective-permute-done((bf16[2,128,512]{2,1,0:T(8,128)(2,1)S(1)}, bf16[2,128,512]{2,1,0:T(8,128)(2,1)S(1)}, u32[]{:S(2)}, u32[]{:S(2)}) %collective-permute-start) | collective-permute-done | bytes 262176 | tf_op jit(solution)/shard_map/ppermute | solution.py:265
  25.4 3.7 %all-gather.1 = bf16[4,128,512]{2,1,0:T(8,128)(2,1)S(1)} all-gather(bf16[2,128,512]{2,1,0:T(8,128)(2,1)S(1)} %collective-permute-done), channel_id=3, replica_groups=mesh['group'=4,'pair'=2,'core'=2,'ctx'=32] {'core'}, dimensions={0}, use_global_device_ids=true | all-gather | bytes 786432 | tf_op jit(solution)/shard_map/all_gather | solution.py:267
  29.0 1.8 %all-to-all-done.kv = bf16[32,64,128]{2,1,0:T(8,128)(2,1)S(1)} async-done(((bf16[32,64,128]{2,1,0:T(8,128)(2,1)}), bf16[32,64,128]{2,1,0:T(8,128)(2,1)S(1)}, u32[]{:S(2)}, u32[]{:S(2)}) %all-to-all-start) | async-done | bytes 524320 | tf_op jit(solution)/shard_map/all_to_all | solution.py:256
  30.8 2.7 %shard_map.78 = f32[8,1024]{1,0:T(8,128)S(1)} custom-call(s32[2,32]{1,0:T(2,128)S(1)} %get-tuple-element.12.spans, bf16[32,64,128]{2,1,0:T(8,128)(2,1)S(1)} %all-to-all-done.kv, bf16[2,2,128,512]{3,2,1,0:T(8,128)(2,1)S(1)} %bitcast.7, bf16[2,2,128,512]{3,2,1,0:T(8,128)(2,1)S(1)} %bitcast.9), custom_call_target="tpu_custom_call" | custom-call | flops 1073741824 | bytes 1048576 | tf_op jit(solution)/shard_map/pallas_call | solution.py:230
  33.6 8.8 %all-gather.2 = f32[32,1024]{1,0:T(8,128)S(1)} all-gather(f32[8,1024]{1,0:T(8,128)S(1)} %shard_map.78), channel_id=4, replica_groups=mesh['group'=4,'pair'=2,'core'=2,'ctx'=32] {'pair','core'}, dimensions={0}, use_global_device_ids=true | all-gather | bytes 163840 | tf_op jit(solution)/shard_map/all_gather | solution.py:280
  42.3 5.6 %shard_map.79 = (bf16[32,64,128]{2,1,0:T(8,128)(2,1)}, bf16[128,512]{1,0:T(8,128)(2,1)S(1)}, bf16[128,512]{1,0:T(8,128)(2,1)S(1)}, bf16[128,512]{1,0:T(8,128)(2,1)S(1)}, bf16[128,512]{1,0:T(8,128)(2,1)S(1)}) custom-call(s32[2,32]{1,0:T(2,128)S(1)} %get-tuple-element.12.spans, f32[4,8,1024]{2,1,0:T(8,128)S(1)} %bitcast.12, ...), custom_call_target="tpu_custom_call" | custom-call | flops 2147483648 | bytes 1048576 | tf_op jit(solution)/shard_map/pallas_call | solution.py:230
  47.9 4.7 %all-to-all-start.1 = ((bf16[32,64,128]{2,1,0:T(8,128)(2,1)}), bf16[32,64,128]{2,1,0:T(8,128)(2,1)S(1)}, u32[]{:S(2)}, u32[]{:S(2)}) async-start(bf16[32,64,128]{2,1,0:T(8,128)(2,1)} %get-tuple-element.18), calls=%async_computation.1 | async-start | bytes 1048576 | tf_op jit(solution)/shard_map/all_to_all | solution.py:300
  52.6 2.4 %collective-permute-start.1 = (bf16[128,512]{1,0:T(8,128)(2,1)S(1)}, bf16[128,512]{1,0:T(8,128)(2,1)S(1)}, u32[]{:S(2)}, u32[]{:S(2)}) collective-permute-start(bf16[128,512]{1,0:T(8,128)(2,1)S(1)} %get-tuple-element.15), channel_id=1, source_target_pairs={{0,32},{32,0},{64,96},{96,64},{1,33},{33,1},{65,97},{97,65},{2,34}... | collective-permute-start | bytes 393224 | tf_op jit(solution)/shard_map/ppermute | solution.py:303
  55.0 3.1 %collective-permute-start.2 = (bf16[128,512]{1,0:T(8,128)(2,1)S(1)}, bf16[128,512]{1,0:T(8,128)(2,1)S(1)}, u32[]{:S(2)}, u32[]{:S(2)}) collective-permute-start(bf16[128,512]{1,0:T(8,128)(2,1)S(1)} %get-tuple-element.16), channel_id=1, source_target_pairs={{0,64},{32,96},{64,0},{96,32},{1,65},{33,97},{65,1},{97,33},{2,66}... | collective-permute-start | bytes 393224 | tf_op jit(solution)/shard_map/ppermute | solution.py:303
  58.1 2.4 %collective-permute-start.3 = (bf16[128,512]{1,0:T(8,128)(2,1)S(1)}, bf16[128,512]{1,0:T(8,128)(2,1)S(1)}, u32[]{:S(2)}, u32[]{:S(2)}) collective-permute-start(bf16[128,512]{1,0:T(8,128)(2,1)S(1)} %get-tuple-element.17), channel_id=1, source_target_pairs={{0,96},{32,64},{64,32},{96,0},{1,97},{33,65},{65,33},{97,1},{2,98}... | collective-permute-start | bytes 393224 | tf_op jit(solution)/shard_map/ppermute | solution.py:303
  60.5 0.0 collective-permute-done.1
  60.5 1.4 %collective-permute-done.2 = bf16[128,512]{1,0:T(8,128)(2,1)S(1)} collective-permute-done((bf16[128,512]{1,0:T(8,128)(2,1)S(1)}, bf16[128,512]{1,0:T(8,128)(2,1)S(1)}, u32[]{:S(2)}, u32[]{:S(2)}) %collective-permute-start.2) | collective-permute-done | bytes 131104 | tf_op jit(solution)/shard_map/ppermute | solution.py:303
  61.9 3.8 %collective-permute-done.3 = bf16[128,512]{1,0:T(8,128)(2,1)S(1)} collective-permute-done((bf16[128,512]{1,0:T(8,128)(2,1)S(1)}, bf16[128,512]{1,0:T(8,128)(2,1)S(1)}, u32[]{:S(2)}, u32[]{:S(2)}) %collective-permute-start.3) | collective-permute-done | bytes 131104 | tf_op jit(solution)/shard_map/ppermute | solution.py:303
  65.8 0.7 add_convert_fusion
  66.5 1.8 %all-to-all-done.1 = bf16[32,64,128]{2,1,0:T(8,128)(2,1)S(1)} async-done(((bf16[32,64,128]{2,1,0:T(8,128)(2,1)}), bf16[32,64,128]{2,1,0:T(8,128)(2,1)S(1)}, u32[]{:S(2)}, u32[]{:S(2)}) %all-to-all-start.1) | async-done | bytes 524320 | tf_op jit(solution)/shard_map/all_to_all | solution.py:300
  68.3 0.1 reduce_sum.12
  68.4 7.3 %all-gather.3 = bf16[256,128]{1,0:T(8,128)(2,1)S(1)} all-gather(bf16[64,128]{1,0:T(8,128)(2,1)S(1)} %reduce_sum.12), channel_id=5, replica_groups=mesh['group'=4,'pair'=2,'core'=2,'ctx'=32] {'pair','core'}, dimensions={0}, use_global_device_ids=true | all-gather | bytes 81920 | tf_op jit(solution)/shard_map/all_gather | solution.py:306
  75.7 0.7 shard_map.80
  (1 shorter events, 0.0 us)
Async XLA Ops:
  2.3 13.7 %copy-start = (bf16[128,512]{1,0:T(8,128)(2,1)S(1)}, bf16[128,512]{1,0:T(8,128)(2,1)}, u32[]{:S(2)}) copy-start(bf16[128,512]{1,0:T(8,128)(2,1)} %queries.1) | copy-start | bytes 393220
  2.3 13.7 %copy-start.1 = (bf16[128,512]{1,0:T(8,128)(2,1)S(1)}, bf16[128,512]{1,0:T(8,128)(2,1)}, u32[]{:S(2)}) copy-start(bf16[128,512]{1,0:T(8,128)(2,1)} %cotan.1) | copy-start | bytes 393220
  2.3 28.5 %all-to-all-start = ((bf16[32,64,128]{2,1,0:T(8,128)(2,1)}), bf16[32,64,128]{2,1,0:T(8,128)(2,1)S(1)}, u32[]{:S(2)}, u32[]{:S(2)}) async-start(bf16[32,64,128]{2,1,0:T(8,128)(2,1)} %shard_map.77), calls=%async_computation | async-start | bytes 1048576 | tf_op jit(solution)/shard_map/all_to_all | solution.py:256
  15.9 0.7 copy-start.2
  16.6 8.8 %collective-permute-start = (bf16[2,128,512]{2,1,0:T(8,128)(2,1)S(1)}, bf16[2,128,512]{2,1,0:T(8,128)(2,1)S(1)}, u32[]{:S(2)}, u32[]{:S(2)}) collective-permute-start(bf16[2,128,512]{2,1,0:T(8,128)(2,1)S(1)} %get-tuple-element.13), channel_id=1, source_target_pairs={{0,64},{64,0},{1,65},{65,1},{2,66},{66,2},{3,67},{67,3},{4,68},{68... | collective-permute-start | bytes 786440 | tf_op jit(solution)/shard_map/ppermute | solution.py:265
  47.9 20.4 %all-to-all-start.1 = ((bf16[32,64,128]{2,1,0:T(8,128)(2,1)}), bf16[32,64,128]{2,1,0:T(8,128)(2,1)S(1)}, u32[]{:S(2)}, u32[]{:S(2)}) async-start(bf16[32,64,128]{2,1,0:T(8,128)(2,1)} %get-tuple-element.18), calls=%async_computation.1 | async-start | bytes 1048576 | tf_op jit(solution)/shard_map/all_to_all | solution.py:300
  52.6 7.9 %collective-permute-start.1 = (bf16[128,512]{1,0:T(8,128)(2,1)S(1)}, bf16[128,512]{1,0:T(8,128)(2,1)S(1)}, u32[]{:S(2)}, u32[]{:S(2)}) collective-permute-start(bf16[128,512]{1,0:T(8,128)(2,1)S(1)} %get-tuple-element.15), channel_id=1, source_target_pairs={{0,32},{32,0},{64,96},{96,64},{1,33},{33,1},{65,97},{97,65},{2,34}... | collective-permute-start | bytes 393224 | tf_op jit(solution)/shard_map/ppermute | solution.py:303
  55.0 7.0 %collective-permute-start.2 = (bf16[128,512]{1,0:T(8,128)(2,1)S(1)}, bf16[128,512]{1,0:T(8,128)(2,1)S(1)}, u32[]{:S(2)}, u32[]{:S(2)}) collective-permute-start(bf16[128,512]{1,0:T(8,128)(2,1)S(1)} %get-tuple-element.16), channel_id=1, source_target_pairs={{0,64},{32,96},{64,0},{96,32},{1,65},{33,97},{65,1},{97,33},{2,66}... | collective-permute-start | bytes 393224 | tf_op jit(solution)/shard_map/ppermute | solution.py:303
  58.1 7.6 %collective-permute-start.3 = (bf16[128,512]{1,0:T(8,128)(2,1)S(1)}, bf16[128,512]{1,0:T(8,128)(2,1)S(1)}, u32[]{:S(2)}, u32[]{:S(2)}) collective-permute-start(bf16[128,512]{1,0:T(8,128)(2,1)S(1)} %get-tuple-element.17), channel_id=1, source_target_pairs={{0,96},{32,64},{64,32},{96,0},{1,97},{33,65},{65,33},{97,1},{2,98}... | collective-permute-start | bytes 393224 | tf_op jit(solution)/shard_map/ppermute | solution.py:303

commit v4 on v3

--- a/solution.py
+++ b/solution.py
@@ -64,28 +64,29 @@
 
 def pair_kernel(queries, cotan, spans, out, spans_out):
     spans_out[...] = spans[...]
-    out[0] = queries[...]
-    out[1] = cotan[...]
-
-
-def load(meta, spans, kv, own, other, ks, vs, qs, gs):
+    for which, ref in enumerate((queries, cotan)):
+        for half in range(2):
+            for head in range(ref.shape[1] // HD):
+                rows = slice(half * SPAN, (half + 1) * SPAN)
+                out[which, half, head * SPAN : (head + 1) * SPAN, :] = ref[rows, head * HD : (head + 1) * HD]
+
+
+def piece(own, other, which, half, at):
+    return (own, other)[at // 2][at % 2, which, half]
+
+
+def to_local(meta, rows):
+    middle = rows.shape[1] // 2
+    turned = jnp.concatenate((rows[:, middle:], rows[:, :middle]), axis=1)
+    return jnp.where(meta[4] == 1, turned, rows)
+
+
+def sort_keys(spans, kv, ks, vs):
     for src in range(kv.shape[0]):
         for half in range(2):
             at = pl.multiple_of(spans[half, src] * SUB, SUB)
             ks[pl.ds(at, SUB), :] = kv[src, half * SUB : (half + 1) * SUB, :]
             vs[pl.ds(at, SUB), :] = kv[src, (2 + half) * SUB : (3 + half) * SUB, :]
-    heads = own.shape[3] // HD
-    for pair, ref in enumerate((own, other)):
-        for core in range(2):
-            for head in range(heads):
-                at = (((pair ^ meta[4]) * 2 + core) * heads + head) * SPAN
-                at = pl.multiple_of(at, SPAN)
-                for half in range(2):
-                    rows = slice(half * SPAN, (half + 1) * SPAN)
-                    cols = slice(head * HD, (head + 1) * HD)
-                    rank = half ^ meta[5]
-                    qs[rank, pl.ds(at, SPAN), :] = ref[core, 0, rows, cols]
-                    gs[rank, pl.ds(at, SPAN), :] = ref[core, 1, rows, cols]
 
 
 def offsets():
@@ -113,23 +114,23 @@
 WIDTH = 256
 
 
-def stats_kernel(spans, kv, own, other, out, ks, vs, qs, gs, part, off):
+def stats_kernel(spans, kv, own, other, out, ks, vs, part, off):
     meta = place(spans)
     off[...] = offsets()
-    load(meta, spans, kv, own, other, ks, vs, qs, gs)
-    rows = qs.shape[1]
+    sort_keys(spans, kv, ks, vs)
+    rows = out.shape[1]
     for unit, (half, tile, masked) in enumerate(units(meta)):
         at = pl.multiple_of(tile * TILE, TILE) if unit == 4 else tile * TILE
         key = ks[pl.ds(at, TILE), :]
         value = vs[pl.ds(at, TILE), :]
         for first in range(0, rows, WIDTH):
             cols = slice(first, first + WIDTH)
-            score = dot(key, qs[half, cols, :], NT)
+            score = dot(key, piece(own, other, 0, half ^ meta[5], first // WIDTH), NT)
             if masked:
                 score = jnp.where(off[...] <= bound(meta, half, tile), score, LOW)
             top = jnp.maximum(jnp.max(score, axis=0, keepdims=True), FLOOR)
             weight = jnp.exp2((score - top) * EXP2)
-            dprob = dot(value, gs[half, cols, :], NT)
+            dprob = dot(value, piece(own, other, 1, half ^ meta[5], first // WIDTH), NT)
             part[unit, 0:1, cols] = top
             part[unit, 1:2, cols] = jnp.sum(weight, axis=0, keepdims=True)
             part[unit, 2:3, cols] = jnp.sum(weight * dprob, axis=0, keepdims=True)
@@ -146,71 +147,91 @@
                 factor = jnp.where(extra, factor, 0.0)
             total = total + factor * part[unit, 1:2, :]
             weighted = weighted + factor * part[unit, 2:3, :]
-        out[half * 3 : half * 3 + 1, :] = top
-        out[half * 3 + 1 : half * 3 + 2, :] = total
-        out[half * 3 + 2 : half * 3 + 3, :] = weighted
+        out[half * 3 : half * 3 + 1, :] = to_local(meta, top)
+        out[half * 3 + 1 : half * 3 + 2, :] = to_local(meta, total)
+        out[half * 3 + 2 : half * 3 + 3, :] = to_local(meta, weighted)
     out[6:8, :] = jnp.zeros((2, rows), F32)
 
 
-def grads_kernel(
-    spans, stats, kv, own, other, dkv_out, dq_0, dq_1, dq_2, dq_3,
-    ks, vs, qs, gs, row_stats, probs_b, dscore_b, dk, dv, dq, kt, back, off,
-):
-    meta = place(spans)
-    off[...] = offsets()
-    load(meta, spans, kv, own, other, ks, vs, qs, gs)
-    kt[...] = ks[...].T
-    rows = qs.shape[1]
+def merge_stats(meta, stats, row_stats):
     for half in range(2):
         tops = [stats[src, half * 3 : half * 3 + 1, :] for src in range(4)]
         top = functools.reduce(jnp.maximum, tops)
         factors = [jnp.exp2((one - top) * EXP2) for one in tops]
         total = sum(factors[src] * stats[src, half * 3 + 1 : half * 3 + 2, :] for src in range(4))
         weighted = sum(factors[src] * stats[src, half * 3 + 2 : half * 3 + 3, :] for src in range(4))
-        row_stats[half, 0:1, :] = top
-        row_stats[half, 1:2, :] = 1.0 / total
-        row_stats[half, 2:3, :] = weighted / total
-    dk[3 * TILE :, :] = jnp.zeros((TILE, HD), F32)
-    dv[3 * TILE :, :] = jnp.zeros((TILE, HD), F32)
+        row_stats[half, 0:1, :] = to_local(meta, top)
+        row_stats[half, 1:2, :] = to_local(meta, 1.0 / total)
+        row_stats[half, 2:3, :] = to_local(meta, weighted / total)
+
+
+def unit_grads(meta, ks, vs, own, other, row_stats, off, probs_b, dscore_b):
+    rows = row_stats.shape[2]
     for unit, (half, tile, masked) in enumerate(units(meta)):
         at = pl.multiple_of(tile * TILE, TILE) if unit == 4 else tile * TILE
         key = ks[pl.ds(at, TILE), :]
         value = vs[pl.ds(at, TILE), :]
         for first in range(0, rows, WIDTH):
             cols = slice(first, first + WIDTH)
-            score = dot(key, qs[half, cols, :], NT)
+            score = dot(key, piece(own, other, 0, half ^ meta[5], first // WIDTH), NT)
             if masked:
                 score = jnp.where(off[...] <= bound(meta, half, tile), score, LOW)
             prob = jnp.exp2((score - row_stats[half, 0:1, cols]) * EXP2) * row_stats[half, 1:2, cols]
-            dprob = dot(value, gs[half, cols, :], NT)
+            dprob = dot(value, piece(own, other, 1, half ^ meta[5], first // WIDTH), NT)
             dscore = prob * (dprob - row_stats[half, 2:3, cols])
-            probs_b[unit % 2, :, cols] = prob.astype(BF16)
+            if probs_b is not None:
+                probs_b[unit % 2, :, cols] = prob.astype(BF16)
             dscore_b[unit % 2, :, cols] = dscore.astype(BF16)
-        dv_tile = dot(probs_b[unit % 2], gs[half])
-        dk_tile = dot(dscore_b[unit % 2], qs[half])
+        yield unit, half, at
+
+
+def key_grads_kernel(
+    spans, stats, ks, vs, own, other, dkv_out, row_stats, probs_b, dscore_b, dk, dv, off
+):
+    meta = place(spans)
+    off[...] = offsets()
+    rows = row_stats.shape[2]
+    merge_stats(meta, stats, row_stats)
+    dk[3 * TILE :, :] = jnp.zeros((TILE, HD), F32)
+    dv[3 * TILE :, :] = jnp.zeros((TILE, HD), F32)
+    for unit, half, at in unit_grads(meta, ks, vs, own, other, row_stats, off, probs_b, dscore_b):
+        keys_of = pl.ds(at, TILE)
+        for which, ref, acc in ((1, probs_b, dv), (0, dscore_b, dk)):
+            part = sum(
+                dot(ref[unit % 2, :, first : first + WIDTH], piece(own, other, which, half ^ meta[5], first // WIDTH))
+                for first in range(0, rows, WIDTH)
+            )
+            if unit in (0, 2, 3):
+                acc[keys_of, :] = part
+            else:
+                acc[keys_of, :] += part
+    for dest in range(dkv_out.shape[0]):
+        for half in range(2):
+            at = pl.multiple_of(spans[half, dest] * SUB, SUB)
+            dkv_out[dest, half * SUB : (half + 1) * SUB, :] = (dk[pl.ds(at, SUB), :] * SCALE).astype(BF16)
+            dkv_out[dest, (2 + half) * SUB : (3 + half) * SUB, :] = dv[pl.ds(at, SUB), :].astype(BF16)
+
+
+def query_grads_kernel(
+    spans, stats, ks, vs, own, other, dq_0, dq_1, dq_2, dq_3, row_stats, dscore_b, dq, kt, back, off
+):
+    meta = place(spans)
+    off[...] = offsets()
+    merge_stats(meta, stats, row_stats)
+    kt[...] = ks[...].T
+    for unit, half, at in unit_grads(meta, ks, vs, own, other, row_stats, off, None, dscore_b):
         dq_half = dot(kt[:, pl.ds(at, TILE)], dscore_b[unit % 2])
-        keys_of = pl.ds(at, TILE)
-        if unit in (0, 2, 3):
-            dv[keys_of, :] = dv_tile
-            dk[keys_of, :] = dk_tile
-        else:
-            dv[keys_of, :] += dv_tile
-            dk[keys_of, :] += dk_tile
         if unit in (0, 1):
             dq[half] = dq_half
         else:
             dq[half] += dq_half
-    for dest in range(dkv_out.shape[0]):
-        for half in range(2):
-            at = pl.multiple_of(spans[half, dest] * SUB, SUB)
-            dkv_out[dest, half * SUB : (half + 1) * SUB, :] = (dk[pl.ds(at, SUB), :] * SCALE).astype(BF16)
-            dkv_out[dest, (2 + half) * SUB : (3 + half) * SUB, :] = dv[pl.ds(at, SUB), :].astype(BF16)
     heads = dq_0.shape[1] // HD
     for half in range(2):
         back[...] = (dq[half ^ meta[5]] * SCALE).T.astype(BF16)
         for step, out in enumerate((dq_0, dq_1, dq_2, dq_3)):
             for head in range(heads):
-                at = pl.multiple_of(((meta[1] ^ step) * heads + head) * SPAN, SPAN)
+                sharer = step - step % 2 + ((meta[1] & 1) ^ (step % 2))
+                at = pl.multiple_of((sharer * heads + head) * SPAN, SPAN)
                 out[half * SPAN : (half + 1) * SPAN, head * HD : (head + 1) * HD] = back[pl.ds(at, SPAN), :]
 
 
@@ -254,9 +275,10 @@
         limit=60,
     )
     kv = lax.all_to_all(kv_send, "ctx", 0, 0, tiled=True)
+    heads = width // HD
     qd, spans = call(
         pair_kernel,
-        (sds((2, rows, width), BF16), sds(spans.shape, jnp.int32)),
+        (sds((2, 2, heads * SPAN, HD), BF16), sds(spans.shape, jnp.int32)),
         [],
         1 << 20,
         "vvv",
@@ -265,39 +287,45 @@
     crossed = lax.ppermute(qd, "pair", [(0, 1), (1, 0)])
     own = lax.all_gather(qd, "core", axis=0)
     other = lax.all_gather(crossed, "core", axis=0)
-    stacked = 2 * 2 * (width // HD) * SPAN
+    stacked = 2 * 2 * heads * SPAN
     keys_held = 2 * ctx_count * SUB
-    common = [VM((keys_held, HD), BF16)] * 2 + [VM((2, stacked, HD), BF16)] * 2
+    held = sds((keys_held, HD), BF16)
     mask = VM((TILE, WIDTH), jnp.int32)
-    stats = call(
+    stats, ks, vs = call(
         stats_kernel,
-        sds((8, stacked), F32),
-        common + [VM((5, 8, stacked), F32), mask],
+        (sds((8, stacked), F32), held, held),
+        [VM((5, 8, stacked), F32), mask],
         1 << 30,
         "svvv",
         spans, kv, own, other,
     )
     stats_all = lax.all_gather(stats, ("pair", "core"), axis=0)
-    dkv_send, dq_mine, *dq_send = call(
-        grads_kernel,
-        (blocks,) + (sds((rows, width), BF16),) * 4,
-        common
-        + [
-            VM((2, 8, stacked), F32),
-            VM((2, TILE, stacked), BF16),
-            VM((2, TILE, stacked), BF16),
-            VM((keys_held, HD), F32),
-            VM((keys_held, HD), F32),
+    tiles = VM((2, TILE, stacked), BF16)
+    row_stats = VM((2, 8, stacked), F32)
+    dkv_send = call(
+        key_grads_kernel,
+        blocks,
+        [row_stats, tiles, tiles, VM((keys_held, HD), F32), VM((keys_held, HD), F32), mask],
+        1 << 31,
+        "svvvvv",
+        spans, stats_all, ks, vs, own, other,
+    )
+    dkv = lax.all_to_all(dkv_send, "ctx", 0, 0, tiled=True)
+    dq_mine, *dq_send = call(
+        query_grads_kernel,
+        (sds((rows, width), BF16),) * 4,
+        [
+            row_stats,
+            tiles,
             VM((2, HD, stacked), F32),
             VM((HD, keys_held), BF16),
             VM((stacked, HD), BF16),
             mask,
         ],
         1 << 31,
-        "svvvv",
-        spans, stats_all, kv, own, other,
-    )
-    dkv = lax.all_to_all(dkv_send, "ctx", 0, 0, tiled=True)
+        "svvvvv",
+        spans, stats_all, ks, vs, own, other,
+    )
     grad_queries = dq_mine.astype(F32)
     for step, piece in enumerate(dq_send, 1):
         grad_queries += lax.ppermute(piece, ("pair", "core"), [(i, i ^ step) for i in range(4)]).astype(F32)

time: 76.9 us -> 76.1 us (0.990)
  waiting for transfers between devices: 11.4 us -> 7.93 us
  Pallas kernels: 10.7 us -> 13.4 us
    ppermute x3, waiting for transfers between devices: 5.25 us -> 2.51 us  [on_device(): lax.ppermute(piece, ('pair', 'core'), [(i, i ^ step) for i in range(4)])]
    pallas_call x5 -> x6, Pallas kernels: 10.7 us -> 13.4 us  [call(): pl.pallas_call(kernel, out_shape=out_shape, in_specs=[pl.BlockSpec(memory...]
  transfers between devices with their start and end apart: 6 -> 6, of which waited for: 5 -> 4; matrix products, arithmetic and copies ran while one was open for 1% -> 1% of each run, Pallas kernels for 0% -> 5%
where the time goes in v4:
time: 76.1 us; the launch traced here: 75.6 us
  starting transfers between devices  29.3 us (39%)
  blocking collectives  22.8 us (30%)
  Pallas kernels  13.4 us (18%)
  waiting for transfers between devices  7.93 us (10%)
  other arithmetic  0.81 us (1%)
    all_to_all x1, starting transfers between devices, on_device(): kv = lax.all_to_all(kv_send, 'ctx', 0, 0, tiled=True)  13.6 us
    pallas_call x6, Pallas kernels, call(): pl.pallas_call(kernel, out_shape=out_shape, in_specs=[pl.BlockSpec(memory...  13.4 us
    all_gather x1, blocking collectives, on_device(): stats_all = lax.all_gather(stats, ('pair', 'core'), axis=0)  8.77 us
    ppermute x3, starting transfers between devices, on_device(): lax.ppermute(piece, ('pair', 'core'), [(i, i ^ step) for i in range(4)])  7.87 us
    all_gather x1, blocking collectives, on_device(): whole = lax.all_gather(summed, ('pair', 'core'), axis=0)  7.31 us
    all_to_all x1, starting transfers between devices, on_device(): dkv = lax.all_to_all(dkv_send, 'ctx', 0, 0, tiled=True)  4.68 us
    all_gather x1, blocking collectives, on_device(): other = lax.all_gather(crossed, 'core', axis=0)  3.66 us
    ppermute x1, starting transfers between devices, on_device(): crossed = lax.ppermute(qd, 'pair', [(0, 1), (1, 0)])  3.12 us
  transfers between devices with their start and end apart: 6, of which 4 were waited for; matrix products, arithmetic and copies ran while one was open for 1% of the time, Pallas kernels for 5%

profile of v4, /device:TPU:1, one launch (start us, length us, event | category | flops | bytes accessed | tf_op | source)
XLA Modules:
  0.0 75.6 jit_solution(467660405086818285)
XLA Ops:
  0.6 1.7 %shard_map.77 = bf16[32,64,128]{2,1,0:T(8,128)(2,1)} custom-call(bf16[128,512]{1,0:T(8,128)(2,1)} %keys.1, bf16[128,512]{1,0:T(8,128)(2,1)} %values.1), custom_call_target="tpu_custom_call" | custom-call | flops 1048576 | bytes 1048576 | tf_op jit(solution)/shard_map/pallas_call | solution.py:251
  2.3 0.0 copy-start
  2.3 0.0 copy-start.1
  2.3 13.6 %all-to-all-start = ((bf16[32,64,128]{2,1,0:T(8,128)(2,1)}), bf16[32,64,128]{2,1,0:T(8,128)(2,1)S(1)}, u32[]{:S(2)}, u32[]{:S(2)}) async-start(bf16[32,64,128]{2,1,0:T(8,128)(2,1)} %shard_map.77), calls=%async_computation | async-start | bytes 1048576 | tf_op jit(solution)/shard_map/all_to_all | solution.py:277
  15.9 0.0 copy-start.2
  16.0 0.0 copy-done
  16.0 0.0 copy-done.1
  16.0 0.7 copy-done.2
  16.7 3.1 %collective-permute-start = (bf16[2,2,256,128]{3,2,1,0:T(8,128)(2,1)S(1)}, bf16[2,2,256,128]{3,2,1,0:T(8,128)(2,1)S(1)}, u32[]{:S(2)}, u32[]{:S(2)}) collective-permute-start(bf16[2,2,256,128]{3,2,1,0:T(8,128)(2,1)S(1)} %get-tuple-element.15), channel_id=1, source_target_pairs={{0,64},{64,0},{1,65},{65,1},{2,66},{66,2},{3,67},{67,3},{4,68},{68... | collective-permute-start | bytes 786440 | tf_op jit(solution)/shard_map/ppermute | solution.py:287
  19.8 3.0 %all-gather = bf16[4,2,256,128]{3,2,1,0:T(8,128)(2,1)S(1)} all-gather(bf16[2,2,256,128]{3,2,1,0:T(8,128)(2,1)S(1)} %get-tuple-element.15), channel_id=2, replica_groups=mesh['group'=4,'pair'=2,'core'=2,'ctx'=32] {'core'}, dimensions={0}, use_global_device_ids=true | all-gather | bytes 786432 | tf_op jit(solution)/shard_map/all_gather | solution.py:288
  22.8 2.6 %collective-permute-done = bf16[2,2,256,128]{3,2,1,0:T(8,128)(2,1)S(1)} collective-permute-done((bf16[2,2,256,128]{3,2,1,0:T(8,128)(2,1)S(1)}, bf16[2,2,256,128]{3,2,1,0:T(8,128)(2,1)S(1)}, u32[]{:S(2)}, u32[]{:S(2)}) %collective-permute-start) | collective-permute-done | bytes 262176 | tf_op jit(solution)/shard_map/ppermute | solution.py:287
  25.4 3.7 %all-gather.1 = bf16[4,2,256,128]{3,2,1,0:T(8,128)(2,1)S(1)} all-gather(bf16[2,2,256,128]{3,2,1,0:T(8,128)(2,1)S(1)} %collective-permute-done), channel_id=3, replica_groups=mesh['group'=4,'pair'=2,'core'=2,'ctx'=32] {'core'}, dimensions={0}, use_global_device_ids=true | all-gather | bytes 786432 | tf_op jit(solution)/shard_map/all_gather | solution.py:289
  29.1 1.8 %all-to-all-done.kv = bf16[32,64,128]{2,1,0:T(8,128)(2,1)S(1)} async-done(((bf16[32,64,128]{2,1,0:T(8,128)(2,1)}), bf16[32,64,128]{2,1,0:T(8,128)(2,1)S(1)}, u32[]{:S(2)}, u32[]{:S(2)}) %all-to-all-start) | async-done | bytes 524320 | tf_op jit(solution)/shard_map/all_to_all | solution.py:277
  30.8 2.7 %shard_map.78 = (f32[8,1024]{1,0:T(8,128)S(1)}, bf16[1024,128]{1,0:T(8,128)(2,1)S(1)}, bf16[1024,128]{1,0:T(8,128)(2,1)S(1)}) custom-call(s32[2,32]{1,0:T(2,128)S(1)} %get-tuple-element.14.spans, bf16[32,64,128]{2,1,0:T(8,128)(2,1)S(1)} %all-to-all-done.kv, bf16[2,2,2,256,128]{4,3,2,1,0:T(8,128)(2,1)S(1)} %bitcast.7, bf16[2,2,2,256,128]{4,3,2,1,0:T(8,128)(2,1)S(1)} %bitcast.10), custom_call_target="tpu_custom_call" | custom-call | flops 1073741824 | bytes 1048576 | tf_op jit(solution)/shard_map/pallas_call | solution.py:251
  33.6 8.8 %all-gather.2 = f32[32,1024]{1,0:T(8,128)S(1)} all-gather(f32[8,1024]{1,0:T(8,128)S(1)} %get-tuple-element.16), channel_id=4, replica_groups=mesh['group'=4,'pair'=2,'core'=2,'ctx'=32] {'pair','core'}, dimensions={0}, use_global_device_ids=true | all-gather | bytes 163840 | tf_op jit(solution)/shard_map/all_gather | solution.py:302
  42.3 4.7 %shard_map.80 = bf16[32,64,128]{2,1,0:T(8,128)(2,1)} custom-call(s32[2,32]{1,0:T(2,128)S(1)} %get-tuple-element.14.spans, f32[4,8,1024]{2,1,0:T(8,128)S(1)} %bitcast.14, bf16[1024,128]{1,0:T(8,128)(2,1)S(1)} %get-tuple-element.17.ks, bf16[1024,128]{1,0:T(8,128)(2,1)S(1)} %get-tuple-element.18.vs, bf16[2,2,2,256,128]{4,3,2,1,0:T(8,128)(2,1)S(1)} %bitcast.8, ...), custom_call_target="tpu_custom_call" | custom-call | flops 2147483648 | bytes 1048576 | tf_op jit(solution)/shard_map/pallas_call | solution.py:251
  47.1 4.7 %all-to-all-start.1 = ((bf16[32,64,128]{2,1,0:T(8,128)(2,1)}), bf16[32,64,128]{2,1,0:T(8,128)(2,1)S(1)}, u32[]{:S(2)}, u32[]{:S(2)}) async-start(bf16[32,64,128]{2,1,0:T(8,128)(2,1)} %shard_map.80), calls=%async_computation.1 | async-start | bytes 1048576 | tf_op jit(solution)/shard_map/all_to_all | solution.py:313
  51.8 3.5 %shard_map.79 = (bf16[128,512]{1,0:T(8,128)(2,1)S(1)}, bf16[128,512]{1,0:T(8,128)(2,1)S(1)}, bf16[128,512]{1,0:T(8,128)(2,1)S(1)}, bf16[128,512]{1,0:T(8,128)(2,1)S(1)}) custom-call(s32[2,32]{1,0:T(2,128)S(1)} %get-tuple-element.14.spans, f32[4,8,1024]{2,1,0:T(8,128)S(1)} %bitcast.15, bf16[1024,128]{1,0:T(8,128)(2,1)S(1)} %get-tuple-element.17.ks, ...), custom_call_target="tpu_custom_call" | custom-call | flops 2147483648 | bytes 1048576 | tf_op jit(solution)/shard_map/pallas_call | solution.py:251
  55.3 3.4 %collective-permute-start.3 = (bf16[128,512]{1,0:T(8,128)(2,1)S(1)}, bf16[128,512]{1,0:T(8,128)(2,1)S(1)}, u32[]{:S(2)}, u32[]{:S(2)}) collective-permute-start(bf16[128,512]{1,0:T(8,128)(2,1)S(1)} %get-tuple-element.22), channel_id=1, source_target_pairs={{0,96},{32,64},{64,32},{96,0},{1,97},{33,65},{65,33},{97,1},{2,98}... | collective-permute-start | bytes 393224 | tf_op jit(solution)/shard_map/ppermute | solution.py:331
  58.7 2.2 %collective-permute-start.2 = (bf16[128,512]{1,0:T(8,128)(2,1)S(1)}, bf16[128,512]{1,0:T(8,128)(2,1)S(1)}, u32[]{:S(2)}, u32[]{:S(2)}) collective-permute-start(bf16[128,512]{1,0:T(8,128)(2,1)S(1)} %get-tuple-element.21), channel_id=1, source_target_pairs={{0,64},{32,96},{64,0},{96,32},{1,65},{33,97},{65,1},{97,33},{2,66}... | collective-permute-start | bytes 393224 | tf_op jit(solution)/shard_map/ppermute | solution.py:331
  60.9 2.3 %collective-permute-start.1 = (bf16[128,512]{1,0:T(8,128)(2,1)S(1)}, bf16[128,512]{1,0:T(8,128)(2,1)S(1)}, u32[]{:S(2)}, u32[]{:S(2)}) collective-permute-start(bf16[128,512]{1,0:T(8,128)(2,1)S(1)} %get-tuple-element.20), channel_id=1, source_target_pairs={{0,32},{32,0},{64,96},{96,64},{1,33},{33,1},{65,97},{97,65},{2,34}... | collective-permute-start | bytes 393224 | tf_op jit(solution)/shard_map/ppermute | solution.py:331
  63.1 0.0 collective-permute-done.3
  63.2 2.5 %collective-permute-done.2 = bf16[128,512]{1,0:T(8,128)(2,1)S(1)} collective-permute-done((bf16[128,512]{1,0:T(8,128)(2,1)S(1)}, bf16[128,512]{1,0:T(8,128)(2,1)S(1)}, u32[]{:S(2)}, u32[]{:S(2)}) %collective-permute-start.2) | collective-permute-done | bytes 131104 | tf_op jit(solution)/shard_map/ppermute | solution.py:331
  65.7 0.0 collective-permute-done.1
  65.7 0.7 add_convert_fusion
  66.4 1.1 %all-to-all-done.1 = bf16[32,64,128]{2,1,0:T(8,128)(2,1)S(1)} async-done(((bf16[32,64,128]{2,1,0:T(8,128)(2,1)}), bf16[32,64,128]{2,1,0:T(8,128)(2,1)S(1)}, u32[]{:S(2)}, u32[]{:S(2)}) %all-to-all-start.1) | async-done | bytes 524320 | tf_op jit(solution)/shard_map/all_to_all | solution.py:313
  67.5 0.1 reduce_sum.12
  67.6 7.3 %all-gather.3 = bf16[256,128]{1,0:T(8,128)(2,1)S(1)} all-gather(bf16[64,128]{1,0:T(8,128)(2,1)S(1)} %reduce_sum.12), channel_id=5, replica_groups=mesh['group'=4,'pair'=2,'core'=2,'ctx'=32] {'pair','core'}, dimensions={0}, use_global_device_ids=true | all-gather | bytes 81920 | tf_op jit(solution)/shard_map/all_gather | solution.py:334
  74.9 0.7 shard_map.81
  (1 shorter events, 0.0 us)
Async XLA Ops:
  2.3 13.7 %copy-start = (bf16[128,512]{1,0:T(8,128)(2,1)S(1)}, bf16[128,512]{1,0:T(8,128)(2,1)}, u32[]{:S(2)}) copy-start(bf16[128,512]{1,0:T(8,128)(2,1)} %queries.1) | copy-start | bytes 393220
  2.3 13.7 %copy-start.1 = (bf16[128,512]{1,0:T(8,128)(2,1)S(1)}, bf16[128,512]{1,0:T(8,128)(2,1)}, u32[]{:S(2)}) copy-start(bf16[128,512]{1,0:T(8,128)(2,1)} %cotan.1) | copy-start | bytes 393220
  2.3 28.5 %all-to-all-start = ((bf16[32,64,128]{2,1,0:T(8,128)(2,1)}), bf16[32,64,128]{2,1,0:T(8,128)(2,1)S(1)}, u32[]{:S(2)}, u32[]{:S(2)}) async-start(bf16[32,64,128]{2,1,0:T(8,128)(2,1)} %shard_map.77), calls=%async_computation | async-start | bytes 1048576 | tf_op jit(solution)/shard_map/all_to_all | solution.py:277
  15.9 0.7 copy-start.2
  16.7 8.8 %collective-permute-start = (bf16[2,2,256,128]{3,2,1,0:T(8,128)(2,1)S(1)}, bf16[2,2,256,128]{3,2,1,0:T(8,128)(2,1)S(1)}, u32[]{:S(2)}, u32[]{:S(2)}) collective-permute-start(bf16[2,2,256,128]{3,2,1,0:T(8,128)(2,1)S(1)} %get-tuple-element.15), channel_id=1, source_target_pairs={{0,64},{64,0},{1,65},{65,1},{2,66},{66,2},{3,67},{67,3},{4,68},{68... | collective-permute-start | bytes 786440 | tf_op jit(solution)/shard_map/ppermute | solution.py:287
  47.1 20.4 %all-to-all-start.1 = ((bf16[32,64,128]{2,1,0:T(8,128)(2,1)}), bf16[32,64,128]{2,1,0:T(8,128)(2,1)S(1)}, u32[]{:S(2)}, u32[]{:S(2)}) async-start(bf16[32,64,128]{2,1,0:T(8,128)(2,1)} %shard_map.80), calls=%async_computation.1 | async-start | bytes 1048576 | tf_op jit(solution)/shard_map/all_to_all | solution.py:313
  55.3 7.9 %collective-permute-start.3 = (bf16[128,512]{1,0:T(8,128)(2,1)S(1)}, bf16[128,512]{1,0:T(8,128)(2,1)S(1)}, u32[]{:S(2)}, u32[]{:S(2)}) collective-permute-start(bf16[128,512]{1,0:T(8,128)(2,1)S(1)} %get-tuple-element.22), channel_id=1, source_target_pairs={{0,96},{32,64},{64,32},{96,0},{1,97},{33,65},{65,33},{97,1},{2,98}... | collective-permute-start | bytes 393224 | tf_op jit(solution)/shard_map/ppermute | solution.py:331
  58.7 7.0 %collective-permute-start.2 = (bf16[128,512]{1,0:T(8,128)(2,1)S(1)}, bf16[128,512]{1,0:T(8,128)(2,1)S(1)}, u32[]{:S(2)}, u32[]{:S(2)}) collective-permute-start(bf16[128,512]{1,0:T(8,128)(2,1)S(1)} %get-tuple-element.21), channel_id=1, source_target_pairs={{0,64},{32,96},{64,0},{96,32},{1,65},{33,97},{65,1},{97,33},{2,66}... | collective-permute-start | bytes 393224 | tf_op jit(solution)/shard_map/ppermute | solution.py:331
  60.9 4.8 %collective-permute-start.1 = (bf16[128,512]{1,0:T(8,128)(2,1)S(1)}, bf16[128,512]{1,0:T(8,128)(2,1)S(1)}, u32[]{:S(2)}, u32[]{:S(2)}) collective-permute-start(bf16[128,512]{1,0:T(8,128)(2,1)S(1)} %get-tuple-element.20), channel_id=1, source_target_pairs={{0,32},{32,0},{64,96},{96,64},{1,33},{33,1},{65,97},{97,65},{2,34}... | collective-permute-start | bytes 393224 | tf_op jit(solution)/shard_map/ppermute | solution.py:331
